TPU v7x, 512 devices: a whole 4x8x8 slice. The times are simulated.
512 devices in a mesh: section: 32 (over z_hi, y, core), expert: 4 (over z_lo), dp: 4 (over x).
Axes of the slice: x: 4, y: 8, z: 8 (z_hi: 2, z_lo: 4; z = z_hi * 4 + z_lo), core: 2. Of those that a mesh axis runs over, the one named last changes fastest.
Arguments:
- section_outputs: bfloat16 [32, 4, 512, 2048], P('section', 'dp', 'expert'), may hold values from -6 to 6
- first_tokens: bfloat16 [4, 512, 2048], P('dp', 'expert'), may hold values from -6 to 6
- kept_layer_inputs: bfloat16 [32, 4, 512, 2048], P('section', 'dp', 'expert'), may hold values from -6 to 6
- section_cotangents: bfloat16 [32, 4, 512, 2048], P('section', 'dp', 'expert'), may hold values from -6 to 6
- loss_cotangent: bfloat16 [4, 512, 2048], P('dp', 'expert'), may hold values from -6 to 6
- norm_gain: float32 [32, 2048], P('section'), may hold values from 0.5 to 1.5
- gate_weights: bfloat16 [32, 768, 2048], P('section', 'expert', 'dp'), may hold values from -0.125 to 0.125
- up_weights: bfloat16 [32, 768, 2048], P('section', 'expert', 'dp'), may hold values from -0.125 to 0.125
- down_weights: bfloat16 [32, 768, 2048], P('section', 'expert', 'dp'), may hold values from -0.21875 to 0.21875
- forward_experts: int32 [32, 4, 512, 8], P('section', 'dp', 'expert'), may hold values from 0 to 127, as said below
- forward_scales: float32 [32, 4, 512, 8], P('section', 'dp', 'expert'), may hold values from 0.05 to 0.6
- backward_experts: int32 [32, 4, 512, 8], P('section', 'dp', 'expert'), may hold values from 0 to 127, as said below
- backward_scales: float32 [32, 4, 512, 8], P('section', 'dp', 'expert'), may hold values from 0.05 to 0.6
Outputs:
- layer_outputs: bfloat16 [32, 4, 512, 2048], P('section', 'dp', 'expert')
- input_grads: bfloat16 [32, 4, 512, 2048], P('section', 'dp', 'expert')
- gate_grads: bfloat16 [32, 768, 2048], P('section', 'expert', 'dp')
- up_grads: bfloat16 [32, 768, 2048], P('section', 'expert', 'dp')
- down_grads: bfloat16 [32, 768, 2048], P('section', 'expert', 'dp')
- gain_grads: float32 [32, 2048], P('section')
Inputs may be any that keep to these rules, and one draw needn't show every extreme that they name: `forward_experts`: each token names 8 different experts. Expert 0 is named by at most 48 of the 128 tokens of one sequence shard; in every draw all 4 shards of some micro-batch of one replica at one section reach 48. `backward_experts`: each token names 8 different experts. Expert 0 is named by at most 48 of the 128 tokens of one sequence shard; in every draw all 4 shards of some micro-batch of one replica at one section reach 48.
All inputs are finite; a program needn't handle non-finite values.
Results may differ from a plain program's by a relative error of at most 0.013.
Values may be sent and summed in bfloat16 or wider, within the bound.
A program may use at most 64 MiB of HBM per device.

v0:
```python
import jax
import jax.numpy as jnp
from jax import lax
from jax.sharding import PartitionSpec as P

CAP = 48


epsilon = 1e-06


def passed_along(block, axis, distance):
    devices = range(lax.axis_size(axis))
    route = [(i - distance, i) for i in devices if i - distance in devices]
    return lax.ppermute(block, axis, route)


def root_square_normalise(values, norm_scale_vector):
    broadened_value = values.astype(jnp.float32)
    inverse_root_scale = lax.rsqrt(
        jnp.mean(broadened_value * broadened_value, axis=-1, keepdims=True) + epsilon
    )
    unit_input_rows = broadened_value * inverse_root_scale
    return (
        unit_input_rows,
        inverse_root_scale,
        (unit_input_rows * norm_scale_vector).astype(jnp.bfloat16),
    )


def tables(chosen, weights):
    picked = chosen == 0
    routed = jnp.any(picked, axis=-1)
    slot_index = jnp.cumsum(routed.astype(jnp.int32)) - 1
    places = jnp.arange(CAP, dtype=jnp.int32)
    routing_table = ((slot_index[None, :] == places[:, None]) & routed[None, :]).astype(jnp.float32)
    route_scale = jnp.sum(jnp.where(picked, weights, jnp.zeros_like(weights)), axis=-1)
    return (routing_table, route_scale)


def along_last(former, latter):
    return lax.dot_general(
        former, latter, (((1,), (1,)), ((), ())), preferred_element_type=jnp.float32
    )


def along_first(former, latter):
    return lax.dot_general(
        former, latter, (((0,), (0,)), ((), ())), preferred_element_type=jnp.float32
    )


def local(
    section_outputs,
    first_tokens,
    kept_layer_inputs,
    section_cotangents,
    loss_cotangent,
    norm_gain,
    gate_weights,
    up_weights,
    down_weights,
    forward_experts,
    forward_scales,
    backward_experts,
    backward_scales,
):
    section_place = lax.axis_index("section")
    norm_scale_vector = norm_gain[0]
    arrived = passed_along(section_outputs[0, 0], "section", 1)
    arriving_gradient = jnp.where(section_place == 0, first_tokens[0], arrived)
    returned = passed_along(section_cotangents[0, 0], "section", -1)
    cotangent = jnp.where(
        section_place == lax.axis_size("section") - 1, loss_cotangent[0], returned
    )
    gate_whole, lift_whole, down_whole = (
        lax.all_gather(gate_weights[0], "dp", axis=1, tiled=True),
        lax.all_gather(up_weights[0], "dp", axis=1, tiled=True),
        lax.all_gather(down_weights[0], "dp", axis=1, tiled=True),
    )
    unit_input_rows, inverse_root_scale, normalised_rows = root_square_normalise(
        arriving_gradient, norm_scale_vector
    )
    routing_table, route_scale = tables(forward_experts[0, 0], forward_scales[0, 0])
    buffer_in = jnp.dot(
        routing_table.astype(jnp.bfloat16), normalised_rows, preferred_element_type=jnp.float32
    ).astype(jnp.bfloat16)
    portion = lax.all_gather(buffer_in, "expert", axis=0, tiled=True)
    gate_act = along_last(portion, gate_whole)
    up_act = along_last(portion, lift_whole)
    hidden = (jax.nn.silu(gate_act) * up_act).astype(jnp.bfloat16)
    partial_value = jnp.dot(hidden, down_whole, preferred_element_type=jnp.float32)
    combined = lax.psum_scatter(
        partial_value.astype(jnp.bfloat16), "expert", scatter_dimension=0, tiled=True
    ).astype(jnp.float32)
    expert_tokens = jnp.dot(routing_table.T, combined, precision=lax.Precision.HIGHEST)
    layer_out = (
        arriving_gradient.astype(jnp.float32) + route_scale[:, None] * expert_tokens
    ).astype(jnp.bfloat16)
    unit_input_rows_back, inverse_root_scale_back, normalised_rows_back = root_square_normalise(
        kept_layer_inputs[0, 0], norm_scale_vector
    )
    table_b, scale_b = tables(backward_experts[0, 0], backward_scales[0, 0])
    cotangent_broad = cotangent.astype(jnp.float32)
    scaled = (scale_b[:, None] * cotangent_broad).astype(jnp.bfloat16)
    table_narrow = table_b.astype(jnp.bfloat16)
    rows_back = jnp.dot(
        table_narrow, normalised_rows_back, preferred_element_type=jnp.float32
    ).astype(jnp.bfloat16)
    rows_grad = jnp.dot(table_narrow, scaled, preferred_element_type=jnp.float32).astype(
        jnp.bfloat16
    )
    group_in, group_grad = (
        lax.all_gather(rows_back, "expert", axis=0, tiled=True),
        lax.all_gather(rows_grad, "expert", axis=0, tiled=True),
    )
    gate_act = along_last(group_in, gate_whole)
    up_act = along_last(group_in, lift_whole)
    squash = jax.nn.sigmoid(gate_act)
    hidden_b = (gate_act * squash * up_act).astype(jnp.bfloat16)
    grad_hidden = along_last(group_grad, down_whole)
    grad_gate = (grad_hidden * up_act * squash * (1.0 + gate_act * (1.0 - squash))).astype(
        jnp.bfloat16
    )
    grad_lift = (grad_hidden * gate_act * squash).astype(jnp.bfloat16)
    normed_part = jnp.dot(grad_gate, gate_whole, preferred_element_type=jnp.float32) + jnp.dot(
        grad_lift, lift_whole, preferred_element_type=jnp.float32
    )
    grad_normed = lax.psum_scatter(
        normed_part.astype(jnp.bfloat16), "expert", scatter_dimension=0, tiled=True
    ).astype(jnp.float32)
    normalised_tokens = jnp.dot(table_b.T, grad_normed, precision=lax.Precision.HIGHEST)
    scale_vector_partial = jnp.sum(normalised_tokens * unit_input_rows_back, axis=0)
    gain_total = lax.psum(scale_vector_partial, ("expert", "dp"))
    unit_input_gradient = normalised_tokens * norm_scale_vector
    inner_product_mean = jnp.mean(
        unit_input_gradient * unit_input_rows_back, axis=-1, keepdims=True
    )
    input_gradient = (
        cotangent_broad
        + inverse_root_scale_back
        * (unit_input_gradient - unit_input_rows_back * inner_product_mean)
    ).astype(jnp.bfloat16)
    local_gate = along_first(grad_gate, group_in)
    local_lift = along_first(grad_lift, group_in)
    local_down = along_first(hidden_b, group_grad)
    summed = (
        lax.psum_scatter(
            local_gate.astype(jnp.bfloat16), "dp", scatter_dimension=1, tiled=True
        ).astype(jnp.float32),
        lax.psum_scatter(
            local_lift.astype(jnp.bfloat16), "dp", scatter_dimension=1, tiled=True
        ).astype(jnp.float32),
        lax.psum_scatter(
            local_down.astype(jnp.bfloat16), "dp", scatter_dimension=1, tiled=True
        ).astype(jnp.float32),
    )
    gate_grad = summed[0].astype(jnp.bfloat16)
    lift_grad = summed[1].astype(jnp.bfloat16)
    down_grad = summed[2].astype(jnp.bfloat16)
    return (
        layer_out[None, None],
        input_gradient[None, None],
        gate_grad[None],
        lift_grad[None],
        down_grad[None],
        gain_total[None],
    )


def solution(mesh):
    placed = (
        P("section", "dp", "expert", None),
        P("dp", "expert", None),
        P("section", "dp", "expert", None),
        P("section", "dp", "expert", None),
        P("dp", "expert", None),
        P("section", None),
        P("section", "expert", "dp"),
        P("section", "expert", "dp"),
        P("section", "expert", "dp"),
        P("section", "dp", "expert", None),
        P("section", "dp", "expert", None),
        P("section", "dp", "expert", None),
        P("section", "dp", "expert", None),
    )
    return jax.shard_map(
        local,
        mesh=mesh,
        in_specs=placed,
        out_specs=(
            P("section", "dp", "expert", None),
            P("section", "dp", "expert", None),
            P("section", "expert", "dp"),
            P("section", "expert", "dp"),
            P("section", "expert", "dp"),
            P("section", None),
        ),
        check_vma=False,
    )
```

profile of v0, /device:TPU:1, one launch (start us, length us, event | category | flops | bytes accessed | tf_op | source)
XLA Modules:
  0.0 266.2 jit_solution(6893168743919819807)
XLA Ops:
  7.3 4.7 %collective-permute-start = (bf16[128,2048]{1,0:T(8,128)(2,1)}, bf16[128,2048]{1,0:T(8,128)(2,1)}, u32[]{:S(2)}, u32[]{:S(2)}) collective-permute-start(bf16[128,2048]{1,0:T(8,128)(2,1)} %bitcast.77), channel_id=1, source_target_pairs={{0,16},{16,32},{32,48},{48,64},{64,80},{80,96},{96,112},{112,128},... | collective-permute-start | bytes 1572872 | tf_op jit(solution)/shard_map/ppermute | solution.py:15
  12.0 6.3 %collective-permute-start.1 = (bf16[128,2048]{1,0:T(8,128)(2,1)}, bf16[128,2048]{1,0:T(8,128)(2,1)S(1)}, u32[]{:S(2)}, u32[]{:S(2)}) collective-permute-start(bf16[128,2048]{1,0:T(8,128)(2,1)} %bitcast.76), channel_id=1, source_target_pairs={{16,0},{32,16},{48,32},{64,48},{80,64},{96,80},{112,96},{128,112},... | collective-permute-start | bytes 1572872 | tf_op jit(solution)/shard_map/ppermute | solution.py:15
  19.4 12.5 %all-gather.1 = bf16[1,192,2048]{2,1,0:T(8,128)(2,1)S(1)} all-gather(bf16[1,192,512]{2,1,0:T(8,128)(2,1)} %param.20), channel_id=3, replica_groups=mesh['section'=32,'expert'=4,'dp'=4] {'dp'}, dimensions={2}, use_global_device_ids=true | all-gather | bytes 983040 | tf_op jit(solution)/shard_map/all_gather | solution.py:78
  31.9 10.6 %all-gather = bf16[1,192,2048]{2,1,0:T(8,128)(2,1)S(1)} all-gather(bf16[1,192,512]{2,1,0:T(8,128)(2,1)} %param.19), channel_id=2, replica_groups=mesh['section'=32,'expert'=4,'dp'=4] {'dp'}, dimensions={2}, use_global_device_ids=true | all-gather | bytes 983040 | tf_op jit(solution)/shard_map/all_gather | solution.py:77
  43.6 17.4 %all_gather.23 = bf16[192,2048]{1,0:T(8,128)(2,1)S(1)} all-gather(bf16[48,2048]{1,0:T(8,128)(2,1)S(1)} %convolution_convert_fusion.4), channel_id=1, replica_groups=mesh['section'=32,'expert'=4,'dp'=4] {'expert'}, dimensions={0}, use_global_device_ids=true | all-gather | bytes 983040 | tf_op jit(solution)/shard_map/all_gather | solution.py:114
  62.0 11.5 %all-gather.2 = bf16[1,192,2048]{2,1,0:T(8,128)(2,1)S(1)} all-gather(bf16[1,192,512]{2,1,0:T(8,128)(2,1)S(1)} %copy-done.16), channel_id=4, replica_groups=mesh['section'=32,'expert'=4,'dp'=4] {'dp'}, dimensions={2}, use_global_device_ids=true | all-gather | bytes 983040 | tf_op jit(solution)/shard_map/all_gather | solution.py:79
  73.8 12.7 %all_gather.22 = bf16[192,2048]{1,0:T(8,128)(2,1)S(1)} all-gather(bf16[48,2048]{1,0:T(8,128)(2,1)S(1)} %convolution_convert_fusion.5), channel_id=1, replica_groups=mesh['section'=32,'expert'=4,'dp'=4] {'expert'}, dimensions={0}, use_global_device_ids=true | all-gather | bytes 983040 | tf_op jit(solution)/shard_map/all_gather | solution.py:115
  87.4 1.3 fusion
  88.8 1.3 fusion.17
  90.1 0.8 copy-done.4
  91.2 13.2 %all_gather.18 = bf16[192,2048]{1,0:T(8,128)(2,1)S(1)} all-gather(bf16[48,2048]{1,0:T(8,128)(2,1)S(1)} %convolution_convert_fusion.6), channel_id=1, replica_groups=mesh['section'=32,'expert'=4,'dp'=4] {'expert'}, dimensions={0}, use_global_device_ids=true | all-gather | bytes 983040 | tf_op jit(solution)/shard_map/all_gather | solution.py:88
  104.4 1.1 fusion.32
  105.5 3.2 %convolution_convert_fusion.3 = bf16[192,2048]{1,0:T(8,128)(2,1)} fusion(bf16[192,2048]{1,0:T(8,128)(2,1)S(1)} %all_gather.18, bf16[1,192,2048]{2,1,0:T(8,128)(2,1)} %copy-done.6, bf16[1,192,2048]{2,1,0:T(8,128)(2,1)S(1)} %all-gather.1, f32[192,192]{1,0:T(8,128)} %fusion.32), kind=kOutput, calls=%fused_computation.5 | convolution fusion | flops 302604288 | bytes 3293184 | tf_op jit(solution)/shard_map/dot_general | solution.py:92
  108.8 1.3 convolution_convert_fusion.2
  110.1 1.3 convolution_convert_fusion.1
  111.5 1.3 convolution_convert_fusion
  112.9 19.6 %reduce-scatter.8.cloned.1.call-done = bf16[48,2048]{1,0:T(8,128)(2,1)} async-done(((bf16[192,2048]{1,0:T(8,128)(2,1)}), bf16[48,2048]{1,0:T(8,128)(2,1)}) %reduce-scatter.8.cloned.1.call-update) | async-done | bytes 196624 | tf_op jit(solution)/shard_map/reduce_scatter | solution.py:129
  132.5 1.5 fusion.15
  134.0 36.8 %psum.7 = f32[1,2048]{1,0:T(1,128)} all-reduce(f32[1,2048]{1,0:T(1,128)S(1)} %bitcast.75), channel_id=1, replica_groups=mesh['section'=32,'expert'=4,'dp'=4] {'expert','dp'}, use_global_device_ids=true, to_apply=%region_15.16 | all-reduce | flops 2048 | bytes 16384 | tf_op jit(solution)/shard_map/psum | solution.py:134
  170.8 2.1 fusion.3
  172.9 1.2 fusion.36
  174.1 23.9 %reduce-scatter.10.cloned.1.call-done = bf16[192,512]{1,0:T(8,128)(2,1)} async-done(((bf16[192,2048]{1,0:T(8,128)(2,1)}), bf16[192,512]{1,0:T(8,128)(2,1)}) %reduce-scatter.10.cloned.1.call-update) | async-done | bytes 196624 | tf_op jit(solution)/shard_map/reduce_scatter | solution.py:148
  198.0 30.9 %reduce-scatter.12.cloned.1.call-done = bf16[192,512]{1,0:T(8,128)(2,1)} async-done(((bf16[192,2048]{1,0:T(8,128)(2,1)}), bf16[192,512]{1,0:T(8,128)(2,1)}) %reduce-scatter.12.cloned.1.call-update) | async-done | bytes 196624 | tf_op jit(solution)/shard_map/reduce_scatter | solution.py:151
  228.9 30.9 %reduce-scatter.14.cloned.1.call-done = bf16[192,512]{1,0:T(8,128)(2,1)} async-done(((bf16[192,2048]{1,0:T(8,128)(2,1)}), bf16[192,512]{1,0:T(8,128)(2,1)}) %reduce-scatter.14.cloned.1.call-update) | async-done | bytes 196624 | tf_op jit(solution)/shard_map/reduce_scatter | solution.py:154
  (87 shorter events, 4.9 us)
Async XLA Ops:
  7.2 35.4 %copy-start.2 = (bf16[1,1,128,2048]{3,2,1,0:T(8,128)(2,1)S(1)}, bf16[1,1,128,2048]{3,2,1,0:T(8,128)(2,1)}, u32[]{:S(2)}) copy-start(bf16[1,1,128,2048]{3,2,1,0:T(8,128)(2,1)} %param.15) | copy-start | bytes 1572868
  7.2 35.6 %copy-start.18 = (f32[1,1,128,8]{2,3,1,0:T(8,128)S(1)}, f32[1,1,128,8]{2,3,1,0:T(8,128)}, u32[]{:S(2)}) copy-start(f32[1,1,128,8]{2,3,1,0:T(8,128)} %param.25) | copy-start | bytes 12292
  7.2 35.6 %copy-start.19 = (s32[1,1,128,8]{2,3,1,0:T(8,128)S(1)}, s32[1,1,128,8]{2,3,1,0:T(8,128)}, u32[]{:S(2)}) copy-start(s32[1,1,128,8]{2,3,1,0:T(8,128)} %param.24) | copy-start | bytes 12292
  7.2 36.1 %copy-start.17 = (f32[1,2048]{1,0:T(1,128)S(1)}, f32[1,2048]{1,0:T(1,128)}, u32[]{:S(2)}) copy-start(f32[1,2048]{1,0:T(1,128)} %param.18) | copy-start | bytes 24580
  7.2 125.3 %reduce-scatter.8.cloned.1.call-start = ((), (), s32[]{:S(2)}) async-start(), calls=%async_computation.6 | async-start | bytes 983040 | tf_op jit(solution)/shard_map/reduce_scatter | solution.py:129
  7.3 81.5 %collective-permute-start = (bf16[128,2048]{1,0:T(8,128)(2,1)}, bf16[128,2048]{1,0:T(8,128)(2,1)}, u32[]{:S(2)}, u32[]{:S(2)}) collective-permute-start(bf16[128,2048]{1,0:T(8,128)(2,1)} %bitcast.77), channel_id=1, source_target_pairs={{0,16},{16,32},{32,48},{48,64},{64,80},{80,96},{96,112},{112,128},... | collective-permute-start | bytes 1572872 | tf_op jit(solution)/shard_map/ppermute | solution.py:15
  12.0 61.4 %collective-permute-start.1 = (bf16[128,2048]{1,0:T(8,128)(2,1)}, bf16[128,2048]{1,0:T(8,128)(2,1)S(1)}, u32[]{:S(2)}, u32[]{:S(2)}) collective-permute-start(bf16[128,2048]{1,0:T(8,128)(2,1)} %bitcast.76), channel_id=1, source_target_pairs={{16,0},{32,16},{48,32},{64,48},{80,64},{96,80},{112,96},{128,112},... | collective-permute-start | bytes 1572872 | tf_op jit(solution)/shard_map/ppermute | solution.py:15
  19.0 71.1 %copy-start.20 = (pred[128]{0:T(512)(128)(4,1)}, pred[128]{0:T(512)(128)(4,1)S(1)}, u32[]{:S(2)}) copy-start(pred[128]{0:T(512)(128)(4,1)S(1)} %reduce_or.18) | copy-start | bytes 388
  42.8 44.1 %copy-start.22 = (f32[128]{0:T(128)}, f32[128]{0:T(128)S(1)}, u32[]{:S(2)}) copy-start(f32[128]{0:T(128)S(1)} %add_rsqrt_fusion) | copy-start | bytes 1540
  42.8 30.6 %copy-start.25 = (pred[128]{0:T(512)(128)(4,1)}, pred[128]{0:T(512)(128)(4,1)S(1)}, u32[]{:S(2)}) copy-start(pred[128]{0:T(512)(128)(4,1)S(1)} %reduce_or.19) | copy-start | bytes 388
  43.2 43.7 %copy-start.24 = (s32[128]{0:T(128)}, s32[128]{0:T(128)S(1)}, u32[]{:S(2)}) copy-start(s32[128]{0:T(128)S(1)} %add_reduce_fusion) | copy-start | bytes 1540
  61.4 12.0 %copy-start.7 = (bf16[1,128,2048]{2,1,0:T(8,128)(2,1)S(1)}, bf16[1,128,2048]{2,1,0:T(8,128)(2,1)}, u32[]{:S(2)}) copy-start(bf16[1,128,2048]{2,1,0:T(8,128)(2,1)} %param.17) | copy-start | bytes 1572868
  73.4 13.5 %copy-start.6 = (bf16[1,192,2048]{2,1,0:T(8,128)(2,1)}, bf16[1,192,2048]{2,1,0:T(8,128)(2,1)S(1)}, u32[]{:S(2)}) copy-start(bf16[1,192,2048]{2,1,0:T(8,128)(2,1)S(1)} %all-gather.2) | copy-start | bytes 2359300
  73.4 13.5 %copy-start.9 = (bf16[128,2048]{1,0:T(8,128)(2,1)}, bf16[128,2048]{1,0:T(8,128)(2,1)S(1)}, u32[]{:S(2)}) copy-start(bf16[128,2048]{1,0:T(8,128)(2,1)S(1)} %collective-permute-done.1) | copy-start | bytes 1572868
  88.7 82.1 %reduce-scatter.6.cloned.1.call-start = ((), (), s32[]{:S(2)}) async-start(), calls=%async_computation.5 | async-start | bytes 983040 | tf_op jit(solution)/shard_map/reduce_scatter | solution.py:93
  108.7 89.3 %reduce-scatter.10.cloned.1.call-start = ((), (), s32[]{:S(2)}) async-start(), calls=%async_computation.7 | async-start | bytes 983040 | tf_op jit(solution)/shard_map/reduce_scatter | solution.py:148
  110.1 118.8 %reduce-scatter.12.cloned.1.call-start = ((), (), s32[]{:S(2)}) async-start(), calls=%async_computation.8 | async-start | bytes 983040 | tf_op jit(solution)/shard_map/reduce_scatter | solution.py:151
  111.5 21.1 %copy-start.3 = (bf16[1,1,128,2048]{3,2,1,0:T(8,128)(2,1)S(1)}, bf16[1,1,128,2048]{3,2,1,0:T(8,128)(2,1)}, u32[]{:S(2)}) copy-start(bf16[1,1,128,2048]{3,2,1,0:T(8,128)(2,1)} %param.15) | copy-start | bytes 1572868
  111.5 148.2 %reduce-scatter.14.cloned.1.call-start = ((), (), s32[]{:S(2)}) async-start(), calls=%async_computation.9 | async-start | bytes 983040 | tf_op jit(solution)/shard_map/reduce_scatter | solution.py:154
  112.8 57.9 %copy-start.5 = (bf16[128,2048]{1,0:T(8,128)(2,1)S(1)}, bf16[128,2048]{1,0:T(8,128)(2,1)}, u32[]{:S(2)}) copy-start(bf16[128,2048]{1,0:T(8,128)(2,1)} %copy-done.4) | copy-start | bytes 1572868
  112.8 57.9 %copy-start.21 = (pred[128]{0:T(512)(128)(4,1)S(1)}, pred[128]{0:T(512)(128)(4,1)}, u32[]{:S(2)}) copy-start(pred[128]{0:T(512)(128)(4,1)} %copy-done.20) | copy-start | bytes 388
  112.9 60.0 %copy-start.8 = (bf16[1,128,2048]{2,1,0:T(8,128)(2,1)S(1)}, bf16[1,128,2048]{2,1,0:T(8,128)(2,1)}, u32[]{:S(2)}) copy-start(bf16[1,128,2048]{2,1,0:T(8,128)(2,1)} %param.17) | copy-start | bytes 1572868
  112.9 60.0 %copy-start.10 = (bf16[128,2048]{1,0:T(8,128)(2,1)S(1)}, bf16[128,2048]{1,0:T(8,128)(2,1)}, u32[]{:S(2)}) copy-start(bf16[128,2048]{1,0:T(8,128)(2,1)} %copy-done.9) | copy-start | bytes 1572868
  112.9 60.0 %copy-start.23 = (f32[128]{0:T(128)S(1)}, f32[128]{0:T(128)}, u32[]{:S(2)}) copy-start(f32[128]{0:T(128)} %copy-done.22) | copy-start | bytes 1540
  (9 other events, 13.6 us)
Sparse Core Ops, SparseCore 0:
  88.8 43.6 reduce-scatter.7
  135.4 32.3 reduce-scatter.5
  171.2 26.7 reduce-scatter.9
  201.3 27.5 reduce-scatter.11
  232.1 27.5 reduce-scatter.13
where the time goes:
time: 267 us; the launch traced here: 266 us
  blocking collectives  115 us (43%)
  waiting for transfers between devices  105 us (39%)
  matrix products  15.5 us (6%)
  between operations  14.1 us (5%)
  starting transfers between devices  11.2 us (4%)
  other arithmetic  4.08 us (2%)
    psum x1, blocking collectives, local(): gain_total = lax.psum(scale_vector_partial, ('expert', 'dp'))  36.8 us
    reduce_scatter x1, waiting for transfers between devices, local(): lax.psum_scatter(local_lift.astype(jnp.bfloat16), 'dp', scatter_dimension...  30.9 us
    reduce_scatter x1, waiting for transfers between devices, local(): lax.psum_scatter(local_down.astype(jnp.bfloat16), 'dp', scatter_dimension...  30.9 us
    reduce_scatter x1, waiting for transfers between devices, local(): lax.psum_scatter(local_gate.astype(jnp.bfloat16), 'dp', scatter_dimension...  23.9 us
    reduce_scatter x1, waiting for transfers between devices, local(): lax.psum_scatter(normed_part.astype(jnp.bfloat16), 'expert', scatter_dime...  19.6 us
    all_gather x1, blocking collectives, local(): lax.all_gather(rows_back, 'expert', axis=0, tiled=True)  17.4 us
    all_gather x1, blocking collectives, local(): portion = lax.all_gather(buffer_in, 'expert', axis=0, tiled=True)  13.2 us
    all_gather x1, blocking collectives, local(): lax.all_gather(rows_grad, 'expert', axis=0, tiled=True)  12.7 us
  transfers between devices with their start and end apart: 7, of which 4 were waited for; matrix products, arithmetic and copies ran while one was open for 7% of the time, Pallas kernels for 0%

commit v1 on v0

v1 whole, which is shorter than its diff:
```python
import jax
import jax.numpy as jnp
from jax import lax
from jax.experimental import pallas as pl
from jax.experimental.pallas import tpu as pltpu
from jax.sharding import PartitionSpec as P

CAP = 48
TOK = 128
D = 2048
HID = 192
DS = 512
EPS = 1e-06
MESH = pl.DeviceIdType.MESH
BF = jnp.bfloat16
F32 = jnp.float32


def dot_tt(a, b):
    return lax.dot_general(a, b, (((0,), (0,)), ((), ())), preferred_element_type=F32)


def dot_nt(a, b):
    return lax.dot_general(a, b, (((1,), (1,)), ((), ())), preferred_element_type=F32)


def dot_nn(a, b):
    return jnp.dot(a, b, preferred_element_type=F32)


def tables(chosen, weights):
    picked = chosen == 0
    routed = jnp.max(picked.astype(F32), axis=1, keepdims=True)
    scale = jnp.sum(jnp.where(picked, weights, 0.0), axis=1, keepdims=True)
    row = lax.broadcasted_iota(jnp.int32, (TOK, TOK), 0)
    col = lax.broadcasted_iota(jnp.int32, (TOK, TOK), 1)
    lower = (col <= row).astype(BF)
    count = dot_nn(lower, jnp.broadcast_to(routed, (TOK, TOK)).astype(BF))[:, :1]
    slot = jnp.where(routed > 0.5, count - 1.0, -1.0)
    place = lax.broadcasted_iota(jnp.int32, (TOK, 4 * CAP), 1)
    place = (
        place
        - CAP * (place >= CAP).astype(jnp.int32)
        - CAP * (place >= 2 * CAP).astype(jnp.int32)
        - CAP * (place >= 3 * CAP).astype(jnp.int32)
    )
    table = jnp.where(slot == place.astype(F32), 1.0, 0.0).astype(BF)
    return table, scale


def inverse_rms(x):
    return lax.rsqrt(jnp.mean(x * x, axis=1, keepdims=True) + EPS)


def sigmoid(v):
    return 1.0 / (1.0 + jnp.exp(-v))


def kernel(
    so_ref, ft_ref, kept_ref, sc_ref, lc_ref, gain_ref, gw_ref, uw_ref, dw_ref, fe_ref, fs_ref, be_ref, bs_ref,
    lo_ref, ig_ref, gg_ref, ug_ref, dg_ref, gt_ref,
    kept, cot, inc, w, rows, part, got, dwst, dwgot, dwout, lo, ig, gst, gout,
    lsem, osem, ssem, srsem, wsend, wrecv, zsend, zrecv, psend, precv, dsend, drecv, gsend, grecv,
):
    s, e, r = lax.axis_index("section"), lax.axis_index("expert"), lax.axis_index("dp")
    last = lax.axis_size("section") - 1
    inner = (e == 1) | (e == 2)
    outer = jnp.logical_not(inner)
    end = jnp.where(e == 1, 0, 3)
    other = 3 - e
    far = 3 - end
    near = jnp.where(e == 0, 1, 2)

    def remote(src, dst, ss, rs, dev):
        return pltpu.make_async_remote_copy(
            src_ref=src, dst_ref=dst, send_sem=ss, recv_sem=rs, device_id=dev, device_id_type=MESH
        )

    xs = [lax.rem(r + d, 4) for d in range(4)]
    zs = [lax.rem(e + d, 4) for d in range(4)]

    own_w = [pltpu.make_async_copy(ref, w.at[a, r], lsem.at[1 + a]) for a, ref in enumerate((gw_ref, uw_ref, dw_ref))]
    load_kept = pltpu.make_async_copy(kept_ref, kept, lsem.at[0])
    load_kept.start()
    barrier = pltpu.get_barrier_semaphore()
    for d in (1, 2, 3):
        pl.semaphore_signal(barrier, inc=1, device_id=(s, e, xs[d]), device_id_type=MESH)
        pl.semaphore_signal(barrier, inc=1, device_id=(s, zs[d], r), device_id_type=MESH)

    @pl.when(s < last)
    def _():
        pl.semaphore_signal(barrier, inc=1, device_id=(s + 1, e, r), device_id_type=MESH)

    @pl.when(s > 0)
    def _():
        pl.semaphore_signal(barrier, inc=1, device_id=(s - 1, e, r), device_id_type=MESH)

    for c in own_w:
        c.start()
    first_in = pltpu.make_async_copy(ft_ref, inc, lsem.at[4])
    loss_in = pltpu.make_async_copy(lc_ref, cot, lsem.at[5])

    @pl.when(s == 0)
    def _():
        first_in.start()

    @pl.when(s == last)
    def _():
        loss_in.start()

    pl.semaphore_wait(barrier, 6 + jnp.where((s > 0) & (s < last), 2, 1))

    hop_cot = remote(sc_ref, cot, ssem.at[0], srsem.at[0], (jnp.maximum(s - 1, 0), e, r))
    hop_inc = remote(so_ref, inc, ssem.at[1], srsem.at[1], (jnp.minimum(s + 1, last), e, r))

    @pl.when(s > 0)
    def _():
        hop_cot.start()

    @pl.when(s < last)
    def _():
        hop_inc.start()

    w_copies = []
    for a, ref in enumerate((gw_ref, uw_ref, dw_ref)):
        for d in (1, 3, 2):
            c = remote(ref, w.at[a, r], wsend.at[a, d], wrecv.at[a, d], (s, e, xs[d]))
            c.start()
            w_copies.append(c)

    def z_copy(a, block, k, dev):
        return remote(rows.at[a, block], rows.at[a, block], zsend.at[a, k], zrecv.at[a, block], (s, dev, r))

    def z_own(a):
        @pl.when(inner)
        def _():
            z_copy(a, e, 0, other).start()
            z_copy(a, e, 1, end).start()

        @pl.when(outer)
        def _():
            z_copy(a, e, 0, near).start()

    def z_pass(a, block, k, dev):
        @pl.when(inner)
        def _():
            c = z_copy(a, block, k, dev)
            c.wait_recv()
            c.start()

    gain = gain_ref[...]
    load_kept.wait()
    x = kept[...].astype(F32)
    rscale_b = inverse_rms(x)
    table_b, scale_b = tables(be_ref[...], bs_ref[...])
    pick_b = table_b[:, :CAP]
    rows[0, e] = dot_tt(pick_b, (x * rscale_b * gain).astype(BF)).astype(BF)
    z_own(0)
    table_f, scale_f = tables(fe_ref[...], fs_ref[...])
    z_pass(0, end, 2, other)
    z_pass(0, other, 3, end)

    @pl.when(s == last)
    def _():
        loss_in.wait()

    @pl.when(s < last)
    def _():
        hop_cot.wait_recv()

    rows[1, e] = dot_tt(pick_b, (scale_b * cot[...].astype(F32)).astype(BF)).astype(BF)
    z_own(1)

    @pl.when(s == 0)
    def _():
        first_in.wait()

    @pl.when(s > 0)
    def _():
        hop_inc.wait_recv()

    y = inc[...].astype(F32)
    rows[2, e] = dot_tt(table_f[:, :CAP], (y * inverse_rms(y) * gain).astype(BF)).astype(BF)

    @pl.when(outer)
    def _():
        z_copy(2, e, 0, near).start()

    z_pass(0, far, 4, end)
    z_pass(1, end, 2, other)
    z_pass(1, other, 3, end)

    @pl.when(inner)
    def _():
        z_copy(2, e, 0, other).start()

    z_pass(1, far, 4, end)

    @pl.when(inner)
    def _():
        z_copy(2, e, 1, end).start()

    z_pass(2, end, 2, other)
    z_pass(2, other, 3, end)
    z_pass(2, far, 4, end)

    def z_arrived(a):
        @pl.when(outer)
        def _():
            for d in (1, 2, 3):
                z_copy(a, zs[d], 0, near).wait_recv()

    def w_arrived(a):
        own_w[a].wait()
        for c in w_copies[3 * a : 3 * a + 3]:
            c.wait_recv()

    def project(a, group):
        total = None
        for k in range(4):
            term = dot_nt(group[:, k * DS : (k + 1) * DS], w[a, k])
            total = term if total is None else total + term
        return total

    def send_parts(j):
        for d in (1, 2, 3):
            remote(part.at[j, zs[d]], got.at[j, e], psend.at[j, d], precv.at[j, d], (s, zs[d], r)).start()
        got[j, e] = part[j, e]

    def parts_arrived(j):
        for d in (1, 2, 3):
            c = remote(part.at[j, zs[d]], got.at[j, e], psend.at[j, d], precv.at[j, d], (s, zs[d], r))
            c.wait()

    z_arrived(0)
    w_arrived(0)
    w_arrived(1)
    group_in = rows[0].reshape(4 * CAP, D)
    gate_act = project(0, group_in)
    up_act = project(1, group_in)
    squash = sigmoid(gate_act)
    act = gate_act * squash
    hidden_b = (act * up_act).astype(BF)
    z_arrived(1)
    w_arrived(2)
    group_grad = rows[1].reshape(4 * CAP, D)
    grad_hidden = project(2, group_grad)
    grad_gate = (grad_hidden * up_act * squash * (1.0 + gate_act * (1.0 - squash))).astype(BF)
    grad_up = (grad_hidden * act).astype(BF)
    for k in range(4):
        cols = slice(k * DS, (k + 1) * DS)
        term = dot_nn(grad_gate, w[0, k]) + dot_nn(grad_up, w[1, k])
        part[0, :, :, cols] = term.astype(BF).reshape(4, CAP, DS)
    send_parts(0)

    d_copies = []
    for a, (left, right) in enumerate(((grad_gate, group_in), (grad_up, group_in), (hidden_b, group_grad))):
        for k in range(4):
            dwst[a, k] = dot_tt(left, right[:, k * DS : (k + 1) * DS]).astype(BF)
        for d in (1, 3, 2):
            c = remote(dwst.at[a, xs[d]], dwgot.at[a, r], dsend.at[a, d], drecv.at[a, d], (s, e, xs[d]))
            c.start()
            d_copies.append(c)

    z_arrived(2)
    group = rows[2].reshape(4 * CAP, D)
    g = project(0, group)
    u = project(1, group)
    hidden = (g * sigmoid(g) * u).astype(BF)
    for k in range(4):
        cols = slice(k * DS, (k + 1) * DS)
        part[1, :, :, cols] = dot_nn(hidden, w[2, k]).astype(BF).reshape(4, CAP, DS)
    send_parts(1)

    parts_arrived(0)
    grad_normed = dot_nn(table_b, got[0].reshape(4 * CAP, D))
    xhat = kept[...].astype(F32) * rscale_b
    gst[0, 0] = jnp.sum(grad_normed * xhat, axis=0, keepdims=True)
    gain_z = []
    for d in (1, 2, 3):
        c = remote(gst.at[0, 0], gst.at[0, d], gsend.at[0, d], grecv.at[0, d], (s, zs[d], r))
        c.start()
        gain_z.append(c)
    gx = grad_normed * gain
    mean = jnp.mean(gx * xhat, axis=1, keepdims=True)
    ig[...] = (cot[...].astype(F32) + rscale_b * (gx - xhat * mean)).astype(BF)
    out_ig = pltpu.make_async_copy(ig, ig_ref, osem.at[0])
    out_ig.start()
    for c in gain_z:
        c.wait_recv()
    gst[1, 0] = (gst[0, 0] + gst[0, 1]) + (gst[0, 2] + gst[0, 3])
    gain_x = []
    for d in (1, 2, 3):
        c = remote(gst.at[1, 0], gst.at[1, d], gsend.at[1, d], grecv.at[1, d], (s, e, xs[d]))
        c.start()
        gain_x.append(c)

    parts_arrived(1)
    tokens = dot_nn(table_f, got[1].reshape(4 * CAP, D))
    lo[...] = (inc[...].astype(F32) + scale_f * tokens).astype(BF)
    out_lo = pltpu.make_async_copy(lo, lo_ref, osem.at[1])
    out_lo.start()
    outs = [out_ig, out_lo]

    for a, ref in enumerate((gg_ref, ug_ref, dg_ref)):
        total = dwst[a, r].astype(F32)
        for d in (1, 2, 3):
            d_copies[3 * a + (0, 0, 2, 1)[d]].wait_recv()
        for d in (1, 2, 3):
            total = total + dwgot[a, xs[d]].astype(F32)
        dwout[a] = total.astype(BF)
        c = pltpu.make_async_copy(dwout.at[a], ref, osem.at[2 + a])
        c.start()
        outs.append(c)
    for c in gain_x:
        c.wait_recv()
    gout[...] = (gst[1, 0] + gst[1, 1]) + (gst[1, 2] + gst[1, 3])
    c = pltpu.make_async_copy(gout, gt_ref, osem.at[5])
    c.start()
    outs.append(c)

    @pl.when(s > 0)
    def _():
        hop_cot.wait_send()

    @pl.when(s < last)
    def _():
        hop_inc.wait_send()

    for c in w_copies + d_copies + gain_z + gain_x:
        c.wait_send()
    for a in range(3):
        z_copy(a, e, 0, near).wait_send()

        @pl.when(inner)
        def _():
            for k in range(1, 5):
                z_copy(a, e, k, end).wait_send()

    for c in outs:
        c.wait()


def local(so, ft, kept, sc, lc, gain, gw, uw, dw, fe, fs, be, bs):
    any_spec = pl.BlockSpec(memory_space=pl.ANY)
    vm = pl.BlockSpec(memory_space=pltpu.VMEM)
    dma = pltpu.SemaphoreType.DMA
    outs = pl.pallas_call(
        kernel,
        out_shape=(
            jax.ShapeDtypeStruct((TOK, D), BF),
            jax.ShapeDtypeStruct((TOK, D), BF),
            jax.ShapeDtypeStruct((HID, DS), BF),
            jax.ShapeDtypeStruct((HID, DS), BF),
            jax.ShapeDtypeStruct((HID, DS), BF),
            jax.ShapeDtypeStruct((1, D), F32),
        ),
        in_specs=[any_spec] * 5 + [vm] + [any_spec] * 3 + [vm] * 4,
        out_specs=[any_spec] * 6,
        scratch_shapes=[
            pltpu.VMEM((TOK, D), BF),
            pltpu.VMEM((TOK, D), BF),
            pltpu.VMEM((TOK, D), BF),
            pltpu.VMEM((3, 4, HID, DS), BF),
            pltpu.VMEM((3, 4, CAP, D), BF),
            pltpu.VMEM((2, 4, CAP, D), BF),
            pltpu.VMEM((2, 4, CAP, D), BF),
            pltpu.VMEM((3, 4, HID, DS), BF),
            pltpu.VMEM((3, 4, HID, DS), BF),
            pltpu.VMEM((3, HID, DS), BF),
            pltpu.VMEM((TOK, D), BF),
            pltpu.VMEM((TOK, D), BF),
            pltpu.VMEM((2, 4, 1, D), F32),
            pltpu.VMEM((1, D), F32),
            dma((6,)),
            dma((6,)),
            dma((2,)),
            dma((2,)),
            dma((3, 4)),
            dma((3, 4)),
            dma((3, 5)),
            dma((3, 4)),
            dma((2, 4)),
            dma((2, 4)),
            dma((3, 4)),
            dma((3, 4)),
            dma((2, 4)),
            dma((2, 4)),
        ],
        compiler_params=pltpu.CompilerParams(
            collective_id=0, has_side_effects=True, vmem_limit_bytes=40 << 20
        ),
        name="relay",
    )(
        so.reshape(TOK, D), ft.reshape(TOK, D), kept.reshape(TOK, D), sc.reshape(TOK, D), lc.reshape(TOK, D),
        gain.reshape(1, D), gw[0], uw[0], dw[0], fe[0, 0], fs[0, 0], be[0, 0], bs[0, 0],
    )
    return (
        outs[0][None, None], outs[1][None, None], outs[2][None], outs[3][None], outs[4][None], outs[5],
    )


def solution(mesh):
    tokens = P("section", "dp", "expert", None)
    stored = P("section", "expert", "dp")
    first = P("dp", "expert", None)
    return jax.shard_map(
        local,
        mesh=mesh,
        in_specs=(tokens, first, tokens, tokens, first, P("section", None)) + (stored,) * 3 + (tokens,) * 4,
        out_specs=(tokens, tokens, stored, stored, stored, P("section", None)),
        check_vma=False,
    )
```

time: 267 us -> 110 us (0.41)
  blocking collectives: 115 us -> 0 us
  waiting for transfers between devices: 105 us -> 0 us
  Pallas kernels: 0 us -> 94.2 us
  matrix products: 15.5 us -> 0 us
  between operations: 14.1 us -> 0.68 us
  local copies, waits for them, and re-layouts: 1.28 us -> 14.4 us
  starting transfers between devices: 11.2 us -> 0 us
  other arithmetic: 4.08 us -> 0 us
    reduce_scatter x5 -> x0, waiting for transfers between devices: 105 us -> none  [the longest x1 30.9 us: local(): lax.psum_scatter(local_lift.astype(jnp.bfloat16), 'dp', scatter_dimension...]
    pallas_call x0 -> x1, Pallas kernels: none -> 94.2 us  [local(): pl.pallas_call(kernel, out_shape=(jax.ShapeDtypeStruct((TOK, D), BF), jax...]
    all_gather x6 -> x0, blocking collectives: 78 us -> none  [the longest x1 17.4 us: local(): lax.all_gather(rows_back, 'expert', axis=0, tiled=True)]
    psum x1 -> x0, blocking collectives: 36.8 us -> none  [local(): gain_total = lax.psum(scale_vector_partial, ('expert', 'dp'))]
    dot_general x15 -> x0, matrix products: 15.5 us -> none  [the longest x3 3.87 us: along_first(): lax.dot_general(former, latter, (((0,), (0,)), ((), ())), preferred_eleme...]
    unnamed x52 -> x30, local copies, waits for them, and re-layouts: 1.05 us -> 14.4 us
    ppermute x2 -> x0, starting transfers between devices: 11 us -> none  [passed_along(): return lax.ppermute(block, axis, route)]
  transfers between devices with their start and end apart: 7 -> 0, of which waited for: 4 -> 0; matrix products, arithmetic and copies ran while one was open for 7% -> 0% of each run, Pallas kernels for 0% -> 0%
where the time goes in v1:
time: 110 us; the launch traced here: 109 us
  Pallas kernels  94.2 us (86%)
  local copies, waits for them, and re-layouts  14.4 us (13%)
    pallas_call x1, Pallas kernels, local(): pl.pallas_call(kernel, out_shape=(jax.ShapeDtypeStruct((TOK, D), BF), jax...  94.2 us
    unnamed x30, local copies, waits for them, and re-layouts  14.4 us

profile of v1, /device:TPU:1, one launch (start us, length us, event | category | flops | bytes accessed | tf_op | source)
XLA Modules:
  0.0 109.3 jit_solution(14554187156253447697)
XLA Ops:
  0.6 0.0 copy-start.5
  0.6 0.8 copy.19
  1.5 0.8 copy.20
  2.3 0.0 copy-start.9
  2.3 0.8 copy.21
  3.1 0.0 copy-done.9
  3.1 0.0 copy-start.8
  3.1 0.1 copy.22
  3.2 0.0 copy-done.5
  3.2 0.6 copy-done.8
  3.8 1.0 copy-done
  4.8 1.0 copy-done.1
  5.8 1.0 copy-done.2
  6.9 1.0 copy-done.3
  7.9 1.0 copy-done.4
  9.0 0.9 copy-done.6
  9.9 0.9 copy-done.7
  10.8 94.2 %relay.1 = (bf16[128,2048]{1,0:T(8,128)(2,1)S(1)}, bf16[128,2048]{1,0:T(8,128)(2,1)S(1)}, bf16[192,512]{1,0:T(8,128)(2,1)S(1)}, bf16[192,512]{1,0:T(8,128)(2,1)S...) custom-call(bf16[128,2048]{1,0:T(8,128)(2,1)S(1)} %bitcast.19, bf16[128,2048]{1,0:T(8,128)(2,1)S(1)} %bitcast.20, ...), custom_call_target="tpu_custom_call" | custom-call | tf_op jit(solution)/shard_map/relay/pallas_call | solution.py:348
  105.0 0.8 copy.29
  105.8 0.8 copy.30
  106.6 0.7 copy.31
  107.3 0.7 copy.32
  108.0 0.7 copy.33
  108.7 0.6 copy.34
  (7 shorter events, 0.0 us)
Async XLA Ops:
  0.6 2.5 %copy-start.5 = (bf16[1,192,512]{2,1,0:T(8,128)(2,1)S(1)}, bf16[1,192,512]{2,1,0:T(8,128)(2,1)}, u32[]{:S(2)}) copy-start(bf16[1,192,512]{2,1,0:T(8,128)(2,1)} %param.19) | copy-start | bytes 589828
  2.3 0.8 copy-start.9
  3.1 0.7 copy-start.8
  3.8 1.0 copy-start
  4.8 1.0 copy-start.1
  5.8 1.0 copy-start.2
  6.9 1.0 copy-start.3
  7.9 1.0 copy-start.4
  9.0 0.9 copy-start.6
  9.9 0.9 copy-start.7

commit v2 on v1

--- a/solution.py
+++ b/solution.py
@@ -11,6 +11,8 @@
 HID = 192
 DS = 512
 EPS = 1e-06
+CA = 3
+CR = 3
 MESH = pl.DeviceIdType.MESH
 BF = jnp.bfloat16
 F32 = jnp.float32
@@ -29,6 +31,7 @@
 
 
 def tables(chosen, weights):
+    chosen, weights = chosen.T, weights.T
     picked = chosen == 0
     routed = jnp.max(picked.astype(F32), axis=1, keepdims=True)
     scale = jnp.sum(jnp.where(picked, weights, 0.0), axis=1, keepdims=True)
@@ -59,8 +62,8 @@
 def kernel(
     so_ref, ft_ref, kept_ref, sc_ref, lc_ref, gain_ref, gw_ref, uw_ref, dw_ref, fe_ref, fs_ref, be_ref, bs_ref,
     lo_ref, ig_ref, gg_ref, ug_ref, dg_ref, gt_ref,
-    kept, cot, inc, w, rows, part, got, dwst, dwgot, dwout, lo, ig, gst, gout,
-    lsem, osem, ssem, srsem, wsend, wrecv, zsend, zrecv, psend, precv, dsend, drecv, gsend, grecv,
+    kept, cot, inc, w, rows, part, got, mid, relay, dwst, dwgot, dwout, lo, ig, gst, gout,
+    lsem, osem, ssem, srsem, wsend, wrecv, zsend, zrecv, psend, precv, csend, crecv, rsem, dsend, drecv, gsend, grecv,
 ):
     s, e, r = lax.axis_index("section"), lax.axis_index("expert"), lax.axis_index("dp")
     last = lax.axis_size("section") - 1
@@ -87,13 +90,40 @@
         pl.semaphore_signal(barrier, inc=1, device_id=(s, e, xs[d]), device_id_type=MESH)
         pl.semaphore_signal(barrier, inc=1, device_id=(s, zs[d], r), device_id_type=MESH)
 
-    @pl.when(s < last)
+    from_next = (s < last) & (s != last // 2)
+    from_before = (s > 0) & (s != last // 2 + 1)
+
+    @pl.when(from_next)
     def _():
         pl.semaphore_signal(barrier, inc=1, device_id=(s + 1, e, r), device_id_type=MESH)
 
-    @pl.when(s > 0)
+    @pl.when(from_before)
     def _():
         pl.semaphore_signal(barrier, inc=1, device_id=(s - 1, e, r), device_id_type=MESH)
+
+    half = (last + 1) // 2
+    relays = half // 2
+    up_relay = (s > half) & (lax.rem(s, 2) == 1)
+    down_relay = (s < half) & (lax.rem(s, 2) == 0)
+    relay_at = jnp.where(s > half, s - half, s) // 2
+
+    @pl.when(up_relay)
+    def _():
+        pl.semaphore_signal(barrier, inc=1, device_id=(half - 1, e, r), device_id_type=MESH)
+
+    @pl.when(down_relay)
+    def _():
+        pl.semaphore_signal(barrier, inc=1, device_id=(half, e, r), device_id_type=MESH)
+
+    @pl.when(s == half)
+    def _():
+        for k in range(relays):
+            pl.semaphore_signal(barrier, inc=1, device_id=(half + 1 + 2 * k, e, r), device_id_type=MESH)
+
+    @pl.when(s == half - 1)
+    def _():
+        for k in range(relays):
+            pl.semaphore_signal(barrier, inc=1, device_id=(2 * k, e, r), device_id_type=MESH)
 
     for c in own_w:
         c.start()
@@ -108,18 +138,58 @@
     def _():
         loss_in.start()
 
-    pl.semaphore_wait(barrier, 6 + jnp.where((s > 0) & (s < last), 2, 1))
+    one, none = jnp.int32(1), jnp.int32(0)
+    pl.semaphore_wait(
+        barrier,
+        6
+        + jnp.where(from_next, one, none)
+        + jnp.where(from_before, one, none)
+        + jnp.where(up_relay | down_relay, one, none)
+        + jnp.where((s == half) | (s == half - 1), relays, 0),
+    )
 
     hop_cot = remote(sc_ref, cot, ssem.at[0], srsem.at[0], (jnp.maximum(s - 1, 0), e, r))
     hop_inc = remote(so_ref, inc, ssem.at[1], srsem.at[1], (jnp.minimum(s + 1, last), e, r))
 
-    @pl.when(s > 0)
+    @pl.when(from_before)
     def _():
         hop_cot.start()
 
-    @pl.when(s < last)
+    @pl.when(from_next)
     def _():
         hop_inc.start()
+
+    step = TOK // relays
+
+    def out_by(ref, k, section):
+        return remote(ref.at[pl.ds(k * step, step)], relay, csend.at[k], rsem.at[0], (section, e, r))
+
+    @pl.when(s == half - 1)
+    def _():
+        for k in range(relays):
+            out_by(so_ref, k, half + 1 + 2 * k).start()
+
+    @pl.when(s == half)
+    def _():
+        for k in range(relays):
+            out_by(sc_ref, k, 2 * k).start()
+
+    def in_by(dst, k, section):
+        first = k * step if isinstance(k, int) else pl.multiple_of(k * step, step)
+        return remote(relay, dst.at[pl.ds(first, step)], rsem.at[1], crecv.at[k], (section, e, r))
+
+    def pass_relay():
+        @pl.when(up_relay)
+        def _():
+            c = in_by(inc, relay_at, half)
+            out_by(so_ref, 0, half).wait_recv()
+            c.start()
+
+        @pl.when(down_relay)
+        def _():
+            c = in_by(cot, relay_at, half - 1)
+            out_by(sc_ref, 0, half).wait_recv()
+            c.start()
 
     w_copies = []
     for a, ref in enumerate((gw_ref, uw_ref, dw_ref)):
@@ -128,25 +198,35 @@
             c.start()
             w_copies.append(c)
 
-    def z_copy(a, block, k, dev):
-        return remote(rows.at[a, block], rows.at[a, block], zsend.at[a, k], zrecv.at[a, block], (s, dev, r))
+    ca = CAP // CA
+
+    def z_copy(a, block, k, dev, c):
+        ref = rows.at[a, block, pl.ds(c * ca, ca)]
+        return remote(ref, ref, zsend.at[a, k, c], zrecv.at[a, block, c], (s, dev, r))
+
+    def z_send(a, k, dev):
+        for c in range(CA):
+            z_copy(a, e, k, dev, c).start()
 
     def z_own(a):
         @pl.when(inner)
         def _():
-            z_copy(a, e, 0, other).start()
-            z_copy(a, e, 1, end).start()
+            for c in range(CA):
+                z_copy(a, e, 0, other, c).start()
+                z_copy(a, e, 1, end, c).start()
 
         @pl.when(outer)
         def _():
-            z_copy(a, e, 0, near).start()
-
-    def z_pass(a, block, k, dev):
+            z_send(a, 0, near)
+
+    def z_pass(a, *moves):
         @pl.when(inner)
         def _():
-            c = z_copy(a, block, k, dev)
-            c.wait_recv()
-            c.start()
+            for c in range(CA):
+                for block, k, dev in moves:
+                    copy = z_copy(a, block, k, dev, c)
+                    copy.wait_recv()
+                    copy.start()
 
     gain = gain_ref[...]
     load_kept.wait()
@@ -157,14 +237,19 @@
     rows[0, e] = dot_tt(pick_b, (x * rscale_b * gain).astype(BF)).astype(BF)
     z_own(0)
     table_f, scale_f = tables(fe_ref[...], fs_ref[...])
-    z_pass(0, end, 2, other)
-    z_pass(0, other, 3, end)
+    z_pass(0, (end, 2, other), (other, 3, end))
+    pass_relay()
 
     @pl.when(s == last)
     def _():
         loss_in.wait()
 
-    @pl.when(s < last)
+    @pl.when(s == half - 1)
+    def _():
+        for k in range(relays):
+            in_by(cot, k, half - 1).wait_recv()
+
+    @pl.when(from_next)
     def _():
         hop_cot.wait_recv()
 
@@ -175,7 +260,12 @@
     def _():
         first_in.wait()
 
-    @pl.when(s > 0)
+    @pl.when(s == half)
+    def _():
+        for k in range(relays):
+            in_by(inc, k, half).wait_recv()
+
+    @pl.when(from_before)
     def _():
         hop_inc.wait_recv()
 
@@ -184,31 +274,30 @@
 
     @pl.when(outer)
     def _():
-        z_copy(2, e, 0, near).start()
-
-    z_pass(0, far, 4, end)
-    z_pass(1, end, 2, other)
-    z_pass(1, other, 3, end)
+        z_send(2, 0, near)
+
+    z_pass(0, (far, 4, end))
+    z_pass(1, (end, 2, other), (other, 3, end))
 
     @pl.when(inner)
     def _():
-        z_copy(2, e, 0, other).start()
-
-    z_pass(1, far, 4, end)
+        z_send(2, 0, other)
+
+    z_pass(1, (far, 4, end))
 
     @pl.when(inner)
     def _():
-        z_copy(2, e, 1, end).start()
-
-    z_pass(2, end, 2, other)
-    z_pass(2, other, 3, end)
-    z_pass(2, far, 4, end)
+        z_send(2, 1, end)
+
+    z_pass(2, (end, 2, other), (other, 3, end))
+    z_pass(2, (far, 4, end))
 
     def z_arrived(a):
         @pl.when(outer)
         def _():
             for d in (1, 2, 3):
-                z_copy(a, zs[d], 0, near).wait_recv()
+                for c in range(CA):
+                    z_copy(a, zs[d], 0, near, c).wait_recv()
 
     def w_arrived(a):
         own_w[a].wait()
@@ -222,15 +311,72 @@
             total = term if total is None else total + term
         return total
 
+    cr = CAP // CR
+
+    def leg(j, src, dst, k, m, dev, c):
+        return remote(src, dst.at[pl.ds(c * cr, cr)], psend.at[j, k, c], precv.at[j, m, c], (s, dev, r))
+
+    def for_far(j, c):
+        return leg(j, part.at[j, 3 - e, pl.ds(c * cr, cr)], mid.at[j, 0], 0, 0, near, c)
+
+    def for_across(j, c):
+        return leg(j, part.at[j, 3 - near, pl.ds(c * cr, cr)], mid.at[j, 1], 1, 1, near, c)
+
+    def for_near(j, c):
+        return leg(j, part.at[j, near, pl.ds(c * cr, cr)], got.at[j, 1], 2, 2, near, c)
+
+    def on_far(j, c):
+        return leg(j, part.at[j, far, pl.ds(c * cr, cr)], mid.at[j, 2], 0, 3, other, c)
+
+    def on_other(j, c):
+        return leg(j, part.at[j, other, pl.ds(c * cr, cr)], got.at[j, 2], 1, 4, other, c)
+
+    def on_end(j, c):
+        return leg(j, part.at[j, end, pl.ds(c * cr, cr)], got.at[j, 1], 2, 2, end, c)
+
+    def add_mid(j, dest, m, c):
+        here = pl.ds(c * cr, cr)
+        part[j, dest, here, :] = (part[j, dest, here, :].astype(F32) + mid[j, m, here, :].astype(F32)).astype(BF)
+
     def send_parts(j):
-        for d in (1, 2, 3):
-            remote(part.at[j, zs[d]], got.at[j, e], psend.at[j, d], precv.at[j, d], (s, zs[d], r)).start()
-        got[j, e] = part[j, e]
+        got[j, 0] = part[j, e]
+
+        @pl.when(outer)
+        def _():
+            got[j, 2] = jnp.zeros((CAP, D), BF)
+            for make in (for_far, for_across, for_near):
+                for c in range(CR):
+                    make(j, c).start()
+
+    def pass_parts(j):
+        @pl.when(inner)
+        def _():
+            for c in range(CR):
+                for_far(j, c).wait_recv()
+                add_mid(j, far, 0, c)
+                on_far(j, c).start()
+            for c in range(CR):
+                for_across(j, c).wait_recv()
+                add_mid(j, other, 1, c)
+                on_other(j, c).start()
+            for c in range(CR):
+                on_far(j, c).wait_recv()
+                add_mid(j, end, 2, c)
+                on_end(j, c).start()
 
     def parts_arrived(j):
-        for d in (1, 2, 3):
-            c = remote(part.at[j, zs[d]], got.at[j, e], psend.at[j, d], precv.at[j, d], (s, zs[d], r))
-            c.wait()
+        for c in range(CR):
+            for_near(j, c).wait_recv()
+
+        @pl.when(inner)
+        def _():
+            for c in range(CR):
+                on_other(j, c).wait_recv()
+
+    def parts_sent(j):
+        for k in range(3):
+            for c in range(CR):
+                leg(j, part.at[j, 0, pl.ds(c * cr, cr)], mid.at[j, 0], k, 0, near, c).wait_send()
 
     z_arrived(0)
     w_arrived(0)
@@ -272,8 +418,9 @@
         part[1, :, :, cols] = dot_nn(hidden, w[2, k]).astype(BF).reshape(4, CAP, DS)
     send_parts(1)
 
+    pass_parts(0)
     parts_arrived(0)
-    grad_normed = dot_nn(table_b, got[0].reshape(4 * CAP, D))
+    grad_normed = dot_nn(table_b[:, : 3 * CAP], got[0].reshape(3 * CAP, D))
     xhat = kept[...].astype(F32) * rscale_b
     gst[0, 0] = jnp.sum(grad_normed * xhat, axis=0, keepdims=True)
     gain_z = []
@@ -286,6 +433,7 @@
     ig[...] = (cot[...].astype(F32) + rscale_b * (gx - xhat * mean)).astype(BF)
     out_ig = pltpu.make_async_copy(ig, ig_ref, osem.at[0])
     out_ig.start()
+    pass_parts(1)
     for c in gain_z:
         c.wait_recv()
     gst[1, 0] = (gst[0, 0] + gst[0, 1]) + (gst[0, 2] + gst[0, 3])
@@ -296,7 +444,7 @@
         gain_x.append(c)
 
     parts_arrived(1)
-    tokens = dot_nn(table_f, got[1].reshape(4 * CAP, D))
+    tokens = dot_nn(table_f[:, : 3 * CAP], got[1].reshape(3 * CAP, D))
     lo[...] = (inc[...].astype(F32) + scale_f * tokens).astype(BF)
     out_lo = pltpu.make_async_copy(lo, lo_ref, osem.at[1])
     out_lo.start()
@@ -319,25 +467,52 @@
     c.start()
     outs.append(c)
 
-    @pl.when(s > 0)
+    @pl.when(from_before)
     def _():
         hop_cot.wait_send()
 
-    @pl.when(s < last)
+    @pl.when(from_next)
     def _():
         hop_inc.wait_send()
+
+    @pl.when((s == half) | (s == half - 1))
+    def _():
+        for k in range(relays):
+            out_by(so_ref, k, half).wait_send()
+
+    @pl.when(up_relay | down_relay)
+    def _():
+        in_by(inc, 0, half).wait_send()
+
+    parts_sent(0)
+    parts_sent(1)
 
     for c in w_copies + d_copies + gain_z + gain_x:
         c.wait_send()
     for a in range(3):
-        z_copy(a, e, 0, near).wait_send()
+        for c in range(CA):
+            z_copy(a, e, 0, near, c).wait_send()
 
         @pl.when(inner)
         def _():
             for k in range(1, 5):
-                z_copy(a, e, k, end).wait_send()
+                for c in range(CA):
+                    z_copy(a, e, k, end, c).wait_send()
 
     for c in outs:
+        c.wait()
+
+
+def finish(*refs):
+    ins, outs, held, sems = refs[:6], refs[6:12], refs[12:18], refs[18]
+    loads = [pltpu.make_async_copy(ins[i], held[i], sems.at[0, i]) for i in range(6)]
+    stores = [pltpu.make_async_copy(held[i], outs[i], sems.at[1, i]) for i in range(6)]
+    for c in loads:
+        c.start()
+    for load, store in zip(loads, stores):
+        load.wait()
+        store.start()
+    for c in stores:
         c.wait()
 
 
@@ -364,7 +539,9 @@
             pltpu.VMEM((3, 4, HID, DS), BF),
             pltpu.VMEM((3, 4, CAP, D), BF),
             pltpu.VMEM((2, 4, CAP, D), BF),
-            pltpu.VMEM((2, 4, CAP, D), BF),
+            pltpu.VMEM((2, 3, CAP, D), BF),
+            pltpu.VMEM((2, 3, CAP, D), BF),
+            pltpu.VMEM((16, D), BF),
             pltpu.VMEM((3, 4, HID, DS), BF),
             pltpu.VMEM((3, 4, HID, DS), BF),
             pltpu.VMEM((3, HID, DS), BF),
@@ -378,23 +555,35 @@
             dma((2,)),
             dma((3, 4)),
             dma((3, 4)),
-            dma((3, 5)),
-            dma((3, 4)),
-            dma((2, 4)),
-            dma((2, 4)),
+            dma((3, 5, CA)),
+            dma((3, 4, CA)),
+            dma((2, 3, CR)),
+            dma((2, 5, CR)),
+            dma((8,)),
+            dma((8,)),
+            dma((2,)),
             dma((3, 4)),
             dma((3, 4)),
             dma((2, 4)),
             dma((2, 4)),
         ],
         compiler_params=pltpu.CompilerParams(
-            collective_id=0, has_side_effects=True, vmem_limit_bytes=40 << 20
+            collective_id=0, has_side_effects=True, vmem_limit_bytes=60 << 20
         ),
         name="relay",
     )(
         so.reshape(TOK, D), ft.reshape(TOK, D), kept.reshape(TOK, D), sc.reshape(TOK, D), lc.reshape(TOK, D),
-        gain.reshape(1, D), gw[0], uw[0], dw[0], fe[0, 0], fs[0, 0], be[0, 0], bs[0, 0],
+        gain.reshape(1, D), gw[0], uw[0], dw[0], fe[0, 0].T, fs[0, 0].T, be[0, 0].T, bs[0, 0].T,
     )
+    outs = pl.pallas_call(
+        finish,
+        out_shape=tuple(jax.ShapeDtypeStruct(o.shape, o.dtype) for o in outs),
+        in_specs=[any_spec] * 6,
+        out_specs=[any_spec] * 6,
+        scratch_shapes=[pltpu.VMEM(o.shape, o.dtype) for o in outs] + [dma((2, 6))],
+        compiler_params=pltpu.CompilerParams(vmem_limit_bytes=60 << 20),
+        name="finish",
+    )(*outs)
     return (
         outs[0][None, None], outs[1][None, None], outs[2][None], outs[3][None], outs[4][None], outs[5],
     )

time: 110 us -> 78 us (0.71)
  the two profiles are of different devices: /device:TPU:1 before, /device:TPU:57 now
where the time goes in v2:
time: 78 us; the launch traced here: 77.8 us
  Pallas kernels  77.1 us (99%)
    pallas_call x1, Pallas kernels, local(): pl.pallas_call(kernel, out_shape=(jax.ShapeDtypeStruct((TOK, D), BF), jax...  74.8 us
    pallas_call x1, Pallas kernels, local(): pl.pallas_call(finish, out_shape=tuple((jax.ShapeDtypeStruct(o.shape, o.d...  2.3 us

profile of v2, /device:TPU:57, one launch (start us, length us, event | category | flops | bytes accessed | tf_op | source)
XLA Modules:
  0.0 77.8 jit_solution(8863631652489016658)
XLA Ops:
  0.6 74.8 %relay.1 = (bf16[128,2048]{1,0:T(8,128)(2,1)}, bf16[128,2048]{1,0:T(8,128)(2,1)}, bf16[192,512]{1,0:T(8,128)(2,1)}, bf16[192,512]{1,0:T(8,128)(2,1)}, bf16[192,512]{1,0:T(8,128)(2,1)}, /*index=5*/f32[1,2048]{1,0:T(1,128)}) custom-call(bf16[128,2048]{1,0:T(8,128)(2,1)} %bitcast.25, bf16[128,2048]{1,0:T(8,128)(2,1)} %bitcast.26, bf16[128,2048]{1,0:T(8,128)(2,1)} %bitcast.27, ...), custom_call_target="tpu_custom_call" | custom-call | tf_op jit(solution)/shard_map/relay/pallas_call | solution.py:523
  75.5 2.3 %finish.1 = (bf16[128,2048]{1,0:T(8,128)(2,1)}, bf16[128,2048]{1,0:T(8,128)(2,1)}, bf16[192,512]{1,0:T(8,128)(2,1)}, bf16[192,512]{1,0:T(8,128)(2,1)}, bf16[192,512]{1,0:T(8,128)(2,1)}, /*index=5*/f32[1,2048]{1,0:T(1,128)}) custom-call(bf16[128,2048]{1,0:T(8,128)(2,1)} %get-tuple-element.18.refs_0_, bf16[128,2048]{1,0:T(8,128)(2,1)} %get-tuple-element.19.refs_1_, ...), custom_call_target="tpu_custom_call" | custom-call | tf_op jit(solution)/shard_map/finish/pallas_call | solution.py:578

commit v3 on v2

--- a/solution.py
+++ b/solution.py
@@ -6,6 +6,7 @@
 from jax.sharding import PartitionSpec as P
 
 CAP = 48
+TOP = 8
 TOK = 128
 D = 2048
 HID = 192
@@ -51,6 +52,19 @@
     return table, scale
 
 
+def slots(chosen, weights):
+    picked = chosen == 0
+    routed = jnp.max(picked.astype(F32), axis=0, keepdims=True)
+    scale = jnp.sum(jnp.where(picked, weights, 0.0), axis=0, keepdims=True)
+    row = lax.broadcasted_iota(jnp.int32, (TOK, TOK), 0)
+    col = lax.broadcasted_iota(jnp.int32, (TOK, TOK), 1)
+    upper = (row <= col).astype(BF)
+    count = dot_nn(jnp.broadcast_to(routed, (TOP, TOK)).astype(BF), upper)[:1]
+    slot = jnp.where(routed > 0.5, count - 1.0, -1.0)
+    hit = slot == lax.broadcasted_iota(jnp.int32, (CAP, TOK), 0).astype(F32)
+    return jnp.where(hit, 1.0, 0.0).astype(BF), jnp.sum(jnp.where(hit, scale, 0.0), axis=1, keepdims=True)
+
+
 def inverse_rms(x):
     return lax.rsqrt(jnp.mean(x * x, axis=1, keepdims=True) + EPS)
 
@@ -60,10 +74,10 @@
 
 
 def kernel(
-    so_ref, ft_ref, kept_ref, sc_ref, lc_ref, gain_ref, gw_ref, uw_ref, dw_ref, fe_ref, fs_ref, be_ref, bs_ref,
+    so_ref, ft_ref, kept_ref, sc_ref, lc_ref, gain_in, gw_ref, uw_ref, dw_ref, fe_in, fs_in, be_in, bs_in,
     lo_ref, ig_ref, gg_ref, ug_ref, dg_ref, gt_ref,
-    kept, cot, inc, w, rows, part, got, mid, relay, dwst, dwgot, dwout, lo, ig, gst, gout,
-    lsem, osem, ssem, srsem, wsend, wrecv, zsend, zrecv, psend, precv, csend, crecv, rsem, dsend, drecv, gsend, grecv,
+    fe_ref, fs_ref, be_ref, bs_ref, gain_ref, kept, cot, inc, w, rows, part, got, mid, relay, acts, dwst, dwmid, dwgot, dwout, lo, ig, gst, gout,
+    lsem, osem, ssem, srsem, wsend, wrecv, zsend, zrecv, psend, precv, csend, crecv, rsem, ready, dsend, drecv, gsend, grecv,
 ):
     s, e, r = lax.axis_index("section"), lax.axis_index("expert"), lax.axis_index("dp")
     last = lax.axis_size("section") - 1
@@ -84,11 +98,29 @@
 
     own_w = [pltpu.make_async_copy(ref, w.at[a, r], lsem.at[1 + a]) for a, ref in enumerate((gw_ref, uw_ref, dw_ref))]
     load_kept = pltpu.make_async_copy(kept_ref, kept, lsem.at[0])
+    smalls = [
+        pltpu.make_async_copy(src, dst, lsem.at[6 + i])
+        for i, (src, dst) in enumerate(
+            ((be_in, be_ref), (bs_in, bs_ref), (gain_in, gain_ref), (fe_in, fe_ref), (fs_in, fs_ref))
+        )
+    ]
+    smalls[0].start()
+    smalls[1].start()
     load_kept.start()
+    for c in smalls[2:]:
+        c.start()
     barrier = pltpu.get_barrier_semaphore()
-    for d in (1, 2, 3):
+    for d in (1, 3):
         pl.semaphore_signal(barrier, inc=1, device_id=(s, e, xs[d]), device_id_type=MESH)
-        pl.semaphore_signal(barrier, inc=1, device_id=(s, zs[d], r), device_id_type=MESH)
+
+    @pl.when(outer)
+    def _():
+        pl.semaphore_signal(barrier, inc=1, device_id=(s, near, r), device_id_type=MESH)
+
+    @pl.when(inner)
+    def _():
+        pl.semaphore_signal(barrier, inc=1, device_id=(s, other, r), device_id_type=MESH)
+        pl.semaphore_signal(barrier, inc=1, device_id=(s, end, r), device_id_type=MESH)
 
     from_next = (s < last) & (s != last // 2)
     from_before = (s > 0) & (s != last // 2 + 1)
@@ -107,10 +139,6 @@
     down_relay = (s < half) & (lax.rem(s, 2) == 0)
     relay_at = jnp.where(s > half, s - half, s) // 2
 
-    @pl.when(up_relay)
-    def _():
-        pl.semaphore_signal(barrier, inc=1, device_id=(half - 1, e, r), device_id_type=MESH)
-
     @pl.when(down_relay)
     def _():
         pl.semaphore_signal(barrier, inc=1, device_id=(half, e, r), device_id_type=MESH)
@@ -124,6 +152,7 @@
     def _():
         for k in range(relays):
             pl.semaphore_signal(barrier, inc=1, device_id=(2 * k, e, r), device_id_type=MESH)
+            pl.semaphore_signal(barrier, inc=1, device_id=(half + 1 + 2 * k, e, r), device_id_type=MESH)
 
     for c in own_w:
         c.start()
@@ -141,12 +170,18 @@
     one, none = jnp.int32(1), jnp.int32(0)
     pl.semaphore_wait(
         barrier,
-        6
+        3
+        + jnp.where(inner, one, none)
         + jnp.where(from_next, one, none)
         + jnp.where(from_before, one, none)
-        + jnp.where(up_relay | down_relay, one, none)
-        + jnp.where((s == half) | (s == half - 1), relays, 0),
+        + jnp.where(up_relay, 2, 0)
+        + jnp.where(down_relay, one, none)
+        + jnp.where(s == half, relays, 0),
     )
+
+    @pl.when(up_relay)
+    def _():
+        pl.semaphore_signal(ready, inc=1, device_id=(half - 1, e, r), device_id_type=MESH)
 
     hop_cot = remote(sc_ref, cot, ssem.at[0], srsem.at[0], (jnp.maximum(s - 1, 0), e, r))
     hop_inc = remote(so_ref, inc, ssem.at[1], srsem.at[1], (jnp.minimum(s + 1, last), e, r))
@@ -164,15 +199,17 @@
     def out_by(ref, k, section):
         return remote(ref.at[pl.ds(k * step, step)], relay, csend.at[k], rsem.at[0], (section, e, r))
 
-    @pl.when(s == half - 1)
-    def _():
-        for k in range(relays):
-            out_by(so_ref, k, half + 1 + 2 * k).start()
-
     @pl.when(s == half)
     def _():
         for k in range(relays):
             out_by(sc_ref, k, 2 * k).start()
+
+    def out_up():
+        @pl.when(s == half - 1)
+        def _():
+            pl.semaphore_wait(ready, relays)
+            for k in range(relays):
+                out_by(so_ref, k, half + 1 + 2 * k).start()
 
     def in_by(dst, k, section):
         first = k * step if isinstance(k, int) else pl.multiple_of(k * step, step)
@@ -191,12 +228,42 @@
             out_by(sc_ref, 0, half).wait_recv()
             c.start()
 
-    w_copies = []
-    for a, ref in enumerate((gw_ref, uw_ref, dw_ref)):
-        for d in (1, 3, 2):
-            c = remote(ref, w.at[a, r], wsend.at[a, d], wrecv.at[a, d], (s, e, xs[d]))
-            c.start()
-            w_copies.append(c)
+    right, left = (s, e, xs[1]), (s, e, xs[3])
+    up_half, low_half = pl.ds(0, HID // 2), pl.ds(HID // 2, HID // 2)
+    w_refs = (gw_ref, uw_ref, dw_ref)
+
+    def w_right(a, slot):
+        return remote(w_refs[a], w.at[a, slot], wsend.at[a, 0], wrecv.at[a, 0], right)
+
+    def w_left(a, slot):
+        return remote(w_refs[a], w.at[a, slot], wsend.at[a, 1], wrecv.at[a, 1], left)
+
+    def w_right_on(a, slot):
+        ref = w.at[a, slot, up_half]
+        return remote(ref, ref, wsend.at[a, 2], wrecv.at[a, 2], right)
+
+    def w_left_on(a, slot):
+        ref = w.at[a, slot, low_half]
+        return remote(ref, ref, wsend.at[a, 3], wrecv.at[a, 3], left)
+
+    for a in range(3):
+        w_right(a, r).start()
+        w_left(a, r).start()
+
+    def w_pass(a):
+        w_right(a, xs[3]).wait_recv()
+        w_right_on(a, xs[3]).start()
+        w_left(a, xs[1]).wait_recv()
+        w_left_on(a, xs[1]).start()
+
+    def w_arrived(a):
+        own_w[a].wait()
+        w_right_on(a, xs[2]).wait_recv()
+        w_left_on(a, xs[2]).wait_recv()
+
+    def w_sent(a):
+        for make in (w_right, w_left, w_right_on, w_left_on):
+            make(a, r).wait_send()
 
     ca = CAP // CA
 
@@ -228,17 +295,34 @@
                     copy.wait_recv()
                     copy.start()
 
-    gain = gain_ref[...]
+    def normed_rows(pick, tokens):
+        x = dot_nn(pick, tokens)
+        return (x * inverse_rms(x) * gain_ref[...]).astype(BF)
+
+    smalls[0].wait()
+    smalls[1].wait()
+    pick_b, pick_scale = slots(be_ref[...], bs_ref[...])
     load_kept.wait()
-    x = kept[...].astype(F32)
-    rscale_b = inverse_rms(x)
-    table_b, scale_b = tables(be_ref[...], bs_ref[...])
-    pick_b = table_b[:, :CAP]
-    rows[0, e] = dot_tt(pick_b, (x * rscale_b * gain).astype(BF)).astype(BF)
+    smalls[2].wait()
+    rows[0, e] = normed_rows(pick_b, kept[...])
     z_own(0)
-    table_f, scale_f = tables(fe_ref[...], fs_ref[...])
+    out_up()
+    smalls[3].wait()
+    smalls[4].wait()
+    pick_f, _ = slots(fe_ref[...], fs_ref[...])
     z_pass(0, (end, 2, other), (other, 3, end))
-    pass_relay()
+    w_pass(0)
+
+    late = s == half - 1
+    punctual = jnp.logical_not(late)
+
+    @pl.when(late)
+    def _():
+        w_pass(1)
+        z_pass(0, (far, 4, end))
+        hop_inc.wait_recv()
+        rows[2, e] = normed_rows(pick_f, inc[...])
+        z_own(2)
 
     @pl.when(s == last)
     def _():
@@ -253,8 +337,15 @@
     def _():
         hop_cot.wait_recv()
 
-    rows[1, e] = dot_tt(pick_b, (scale_b * cot[...].astype(F32)).astype(BF)).astype(BF)
+    rows[1, e] = (pick_scale * dot_nn(pick_b, cot[...])).astype(BF)
     z_own(1)
+
+    @pl.when(punctual)
+    def _():
+        w_pass(1)
+        z_pass(0, (far, 4, end))
+
+    pass_relay()
 
     @pl.when(s == 0)
     def _():
@@ -265,51 +356,72 @@
         for k in range(relays):
             in_by(inc, k, half).wait_recv()
 
-    @pl.when(from_before)
+    @pl.when(from_before & punctual)
     def _():
         hop_inc.wait_recv()
 
-    y = inc[...].astype(F32)
-    rows[2, e] = dot_tt(table_f[:, :CAP], (y * inverse_rms(y) * gain).astype(BF)).astype(BF)
-
-    @pl.when(outer)
+    @pl.when(punctual)
+    def _():
+        rows[2, e] = normed_rows(pick_f, inc[...])
+
+    @pl.when(outer & punctual)
     def _():
         z_send(2, 0, near)
 
-    z_pass(0, (far, 4, end))
     z_pass(1, (end, 2, other), (other, 3, end))
-
-    @pl.when(inner)
+    w_pass(2)
+    z_pass(2, (end, 2, other))
+
+    @pl.when(inner & punctual)
     def _():
         z_send(2, 0, other)
 
     z_pass(1, (far, 4, end))
 
-    @pl.when(inner)
-    def _():
-        z_send(2, 1, end)
-
-    z_pass(2, (end, 2, other), (other, 3, end))
-    z_pass(2, (far, 4, end))
-
-    def z_arrived(a):
-        @pl.when(outer)
-        def _():
-            for d in (1, 2, 3):
-                for c in range(CA):
-                    z_copy(a, zs[d], 0, near, c).wait_recv()
-
-    def w_arrived(a):
-        own_w[a].wait()
-        for c in w_copies[3 * a : 3 * a + 3]:
-            c.wait_recv()
+    def z_arrived(a, block):
+        for c in range(CA):
+            z_copy(a, block, 0, near, c).wait_recv()
 
     def project(a, group):
         total = None
         for k in range(4):
-            term = dot_nt(group[:, k * DS : (k + 1) * DS], w[a, k])
-            total = term if total is None else total + term
+            prod = dot_nt(group[:, k * DS : (k + 1) * DS], w[a, k])
+            total = prod if total is None else total + prod
         return total
+
+    def backward_acts(group_in, group_grad):
+        gate_act = project(0, group_in)
+        up_act = project(1, group_in)
+        squash = sigmoid(gate_act)
+        act = gate_act * squash
+        grad_hidden = project(2, group_grad)
+        return (
+            (grad_hidden * up_act * squash * (1.0 + gate_act * (1.0 - squash))).astype(BF),
+            (grad_hidden * act).astype(BF),
+            (act * up_act).astype(BF),
+        )
+
+    def forward_acts(group):
+        g = project(0, group)
+        return (g * sigmoid(g) * project(1, group)).astype(BF)
+
+    def backward_part(grad_gate, grad_up, k):
+        return (dot_nn(grad_gate, w[0, k]) + dot_nn(grad_up, w[1, k])).astype(BF)
+
+    def forward_part(hidden, k):
+        return dot_nn(hidden, w[2, k]).astype(BF)
+
+    def backward_block(block):
+        made = backward_acts(rows[0, block], rows[1, block])
+        for a in range(3):
+            acts[a, block] = made[a]
+        for k in range(4):
+            part[0, block, :, k * DS : (k + 1) * DS] = backward_part(made[0], made[1], k)
+
+    def forward_block(block):
+        hidden = forward_acts(rows[2, block])
+        for k in range(4):
+            part[1, block, :, k * DS : (k + 1) * DS] = forward_part(hidden, k)
 
     cr = CAP // CR
 
@@ -338,31 +450,15 @@
         here = pl.ds(c * cr, cr)
         part[j, dest, here, :] = (part[j, dest, here, :].astype(F32) + mid[j, m, here, :].astype(F32)).astype(BF)
 
-    def send_parts(j):
-        got[j, 0] = part[j, e]
-
-        @pl.when(outer)
-        def _():
-            got[j, 2] = jnp.zeros((CAP, D), BF)
-            for make in (for_far, for_across, for_near):
-                for c in range(CR):
-                    make(j, c).start()
-
-    def pass_parts(j):
-        @pl.when(inner)
-        def _():
-            for c in range(CR):
-                for_far(j, c).wait_recv()
-                add_mid(j, far, 0, c)
-                on_far(j, c).start()
-            for c in range(CR):
-                for_across(j, c).wait_recv()
-                add_mid(j, other, 1, c)
-                on_other(j, c).start()
-            for c in range(CR):
-                on_far(j, c).wait_recv()
-                add_mid(j, end, 2, c)
-                on_end(j, c).start()
+    def pass_term(j, dest, m, arriving, leaving):
+        for c in range(CR):
+            arriving(j, c).wait_recv()
+            add_mid(j, dest, m, c)
+            leaving(j, c).start()
+
+    def send_term(j, make):
+        for c in range(CR):
+            make(j, c).start()
 
     def parts_arrived(j):
         for c in range(CR):
@@ -378,47 +474,106 @@
             for c in range(CR):
                 leg(j, part.at[j, 0, pl.ds(c * cr, cr)], mid.at[j, 0], k, 0, near, c).wait_send()
 
-    z_arrived(0)
-    w_arrived(0)
-    w_arrived(1)
-    group_in = rows[0].reshape(4 * CAP, D)
-    gate_act = project(0, group_in)
-    up_act = project(1, group_in)
-    squash = sigmoid(gate_act)
-    act = gate_act * squash
-    hidden_b = (act * up_act).astype(BF)
-    z_arrived(1)
-    w_arrived(2)
-    group_grad = rows[1].reshape(4 * CAP, D)
-    grad_hidden = project(2, group_grad)
-    grad_gate = (grad_hidden * up_act * squash * (1.0 + gate_act * (1.0 - squash))).astype(BF)
-    grad_up = (grad_hidden * act).astype(BF)
-    for k in range(4):
-        cols = slice(k * DS, (k + 1) * DS)
-        term = dot_nn(grad_gate, w[0, k]) + dot_nn(grad_up, w[1, k])
-        part[0, :, :, cols] = term.astype(BF).reshape(4, CAP, DS)
-    send_parts(0)
-
-    d_copies = []
-    for a, (left, right) in enumerate(((grad_gate, group_in), (grad_up, group_in), (hidden_b, group_grad))):
+    def d_far(a, h):
+        half_rows = (up_half, low_half)[h]
+        return remote(
+            dwst.at[a, xs[2], half_rows], dwmid.at[a, h], dsend.at[a, h], drecv.at[a, h], (right, left)[h]
+        )
+
+    def d_near(a, h, joined):
+        half_rows = (up_half, low_half)[h if joined else 1 - h]
+        n = 2 + 2 * h + (1 if joined else 0)
+        return remote(
+            dwst.at[a, (xs[1], xs[3])[h], half_rows],
+            dwgot.at[a, h, half_rows],
+            dsend.at[a, n],
+            drecv.at[a, n],
+            (right, left)[h],
+        )
+
+    def send_weight_grads():
+        group_in, group_grad = rows[0].reshape(4 * CAP, D), rows[1].reshape(4 * CAP, D)
+        for a, group in enumerate((group_in, group_in, group_grad)):
+            act = acts[a].reshape(4 * CAP, HID)
+            for k in range(4):
+                dwst[a, k] = dot_tt(act, group[:, k * DS : (k + 1) * DS]).astype(BF)
+            for h in range(2):
+                d_far(a, h).start()
+
+    def send_weight_grads_near():
+        for a in range(3):
+            for h in range(2):
+                d_near(a, h, False).start()
+
+    def join_weight_grads():
+        for a in range(3):
+            for h in range(2):
+                d_far(a, h).wait_recv()
+                half_rows, to = (up_half, low_half)[h], (xs[1], xs[3])[h]
+                joined = dwst[a, to, half_rows, :].astype(F32) + dwmid[a, h].astype(F32)
+                dwst[a, to, half_rows, :] = joined.astype(BF)
+                d_near(a, h, True).start()
+
+    gain = gain_ref[...]
+    table_b, scale_b = tables(be_ref[...], bs_ref[...])
+    table_f, scale_f = tables(fe_ref[...], fs_ref[...])
+    rscale_b = inverse_rms(kept[...].astype(F32))
+
+    for a in range(3):
+        w_arrived(a)
+
+    @pl.when(outer)
+    def _():
+        got[0, 2] = jnp.zeros((CAP, D), BF)
+        got[1, 2] = jnp.zeros((CAP, D), BF)
+        for block, make in ((near, for_near), (3 - near, for_across), (3 - e, for_far)):
+            z_arrived(0, block)
+            z_arrived(1, block)
+            backward_block(block)
+            send_term(0, make)
+        backward_block(e)
+        send_weight_grads()
+        for block, make in ((3 - e, for_far), (3 - near, for_across), (near, for_near)):
+            z_arrived(2, block)
+            forward_block(block)
+            send_term(1, make)
+            if make is for_far:
+                send_weight_grads_near()
+            if make is for_across:
+                join_weight_grads()
+        forward_block(e)
+
+    @pl.when(inner)
+    def _():
+        made = backward_acts(rows[0].reshape(4 * CAP, D), rows[1].reshape(4 * CAP, D))
+        for a in range(3):
+            acts[a] = made[a].reshape(4, CAP, HID)
         for k in range(4):
-            dwst[a, k] = dot_tt(left, right[:, k * DS : (k + 1) * DS]).astype(BF)
-        for d in (1, 3, 2):
-            c = remote(dwst.at[a, xs[d]], dwgot.at[a, r], dsend.at[a, d], drecv.at[a, d], (s, e, xs[d]))
-            c.start()
-            d_copies.append(c)
-
-    z_arrived(2)
-    group = rows[2].reshape(4 * CAP, D)
-    g = project(0, group)
-    u = project(1, group)
-    hidden = (g * sigmoid(g) * u).astype(BF)
-    for k in range(4):
-        cols = slice(k * DS, (k + 1) * DS)
-        part[1, :, :, cols] = dot_nn(hidden, w[2, k]).astype(BF).reshape(4, CAP, DS)
-    send_parts(1)
-
-    pass_parts(0)
+            part[0, :, :, k * DS : (k + 1) * DS] = backward_part(made[0], made[1], k).reshape(4, CAP, DS)
+        send_weight_grads()
+
+    z_pass(2, (far, 4, end))
+    z_pass(2, (other, 3, end))
+
+    @pl.when(inner & punctual)
+    def _():
+        z_send(2, 1, end)
+
+    @pl.when(inner)
+    def _():
+        hidden = forward_acts(rows[2].reshape(4 * CAP, D))
+        for k in range(4):
+            part[1, :, :, k * DS : (k + 1) * DS] = forward_part(hidden, k).reshape(4, CAP, DS)
+        send_weight_grads_near()
+        pass_term(0, other, 1, for_across, on_other)
+        join_weight_grads()
+        pass_term(0, far, 0, for_far, on_far)
+        pass_term(0, end, 2, on_far, on_end)
+        pass_term(1, far, 0, for_far, on_far)
+
+    got[0, 0] = part[0, e]
+    got[1, 0] = part[1, e]
+
     parts_arrived(0)
     grad_normed = dot_nn(table_b[:, : 3 * CAP], got[0].reshape(3 * CAP, D))
     xhat = kept[...].astype(F32) * rscale_b
@@ -433,7 +588,12 @@
     ig[...] = (cot[...].astype(F32) + rscale_b * (gx - xhat * mean)).astype(BF)
     out_ig = pltpu.make_async_copy(ig, ig_ref, osem.at[0])
     out_ig.start()
-    pass_parts(1)
+
+    @pl.when(inner)
+    def _():
+        pass_term(1, other, 1, for_across, on_other)
+        pass_term(1, end, 2, on_far, on_end)
+
     for c in gain_z:
         c.wait_recv()
     gst[1, 0] = (gst[0, 0] + gst[0, 1]) + (gst[0, 2] + gst[0, 3])
@@ -451,11 +611,10 @@
     outs = [out_ig, out_lo]
 
     for a, ref in enumerate((gg_ref, ug_ref, dg_ref)):
-        total = dwst[a, r].astype(F32)
-        for d in (1, 2, 3):
-            d_copies[3 * a + (0, 0, 2, 1)[d]].wait_recv()
-        for d in (1, 2, 3):
-            total = total + dwgot[a, xs[d]].astype(F32)
+        for h in range(2):
+            d_near(a, h, False).wait_recv()
+            d_near(a, h, True).wait_recv()
+        total = dwst[a, r].astype(F32) + (dwgot[a, 0].astype(F32) + dwgot[a, 1].astype(F32))
         dwout[a] = total.astype(BF)
         c = pltpu.make_async_copy(dwout.at[a], ref, osem.at[2 + a])
         c.start()
@@ -487,7 +646,13 @@
     parts_sent(0)
     parts_sent(1)
 
-    for c in w_copies + d_copies + gain_z + gain_x:
+    for a in range(3):
+        w_sent(a)
+        for h in range(2):
+            d_far(a, h).wait_send()
+            d_near(a, h, False).wait_send()
+            d_near(a, h, True).wait_send()
+    for c in gain_z + gain_x:
         c.wait_send()
     for a in range(3):
         for c in range(CA):
@@ -518,7 +683,6 @@
 
 def local(so, ft, kept, sc, lc, gain, gw, uw, dw, fe, fs, be, bs):
     any_spec = pl.BlockSpec(memory_space=pl.ANY)
-    vm = pl.BlockSpec(memory_space=pltpu.VMEM)
     dma = pltpu.SemaphoreType.DMA
     outs = pl.pallas_call(
         kernel,
@@ -530,9 +694,14 @@
             jax.ShapeDtypeStruct((HID, DS), BF),
             jax.ShapeDtypeStruct((1, D), F32),
         ),
-        in_specs=[any_spec] * 5 + [vm] + [any_spec] * 3 + [vm] * 4,
+        in_specs=[any_spec] * 13,
         out_specs=[any_spec] * 6,
         scratch_shapes=[
+            pltpu.VMEM((TOP, TOK), jnp.int32),
+            pltpu.VMEM((TOP, TOK), F32),
+            pltpu.VMEM((TOP, TOK), jnp.int32),
+            pltpu.VMEM((TOP, TOK), F32),
+            pltpu.VMEM((1, D), F32),
             pltpu.VMEM((TOK, D), BF),
             pltpu.VMEM((TOK, D), BF),
             pltpu.VMEM((TOK, D), BF),
@@ -542,14 +711,16 @@
             pltpu.VMEM((2, 3, CAP, D), BF),
             pltpu.VMEM((2, 3, CAP, D), BF),
             pltpu.VMEM((16, D), BF),
+            pltpu.VMEM((3, 4, CAP, HID), BF),
             pltpu.VMEM((3, 4, HID, DS), BF),
-            pltpu.VMEM((3, 4, HID, DS), BF),
+            pltpu.VMEM((3, 2, HID // 2, DS), BF),
+            pltpu.VMEM((3, 2, HID, DS), BF),
             pltpu.VMEM((3, HID, DS), BF),
             pltpu.VMEM((TOK, D), BF),
             pltpu.VMEM((TOK, D), BF),
             pltpu.VMEM((2, 4, 1, D), F32),
             pltpu.VMEM((1, D), F32),
-            dma((6,)),
+            dma((11,)),
             dma((6,)),
             dma((2,)),
             dma((2,)),
@@ -562,8 +733,9 @@
             dma((8,)),
             dma((8,)),
             dma((2,)),
-            dma((3, 4)),
-            dma((3, 4)),
+            pltpu.SemaphoreType.REGULAR,
+            dma((3, 6)),
+            dma((3, 6)),
             dma((2, 4)),
             dma((2, 4)),
         ],

time: 78 us -> 69.9 us (0.90)
  Pallas kernels: 77.1 us -> 69.1 us
    pallas_call x1, Pallas kernels: 74.8 us -> 66.8 us  [local(): pl.pallas_call(kernel, out_shape=(jax.ShapeDtypeStruct((TOK, D), BF), jax...]
where the time goes in v3:
time: 69.9 us; the launch traced here: 69.7 us
  Pallas kernels  69.1 us (99%)
    pallas_call x1, Pallas kernels, local(): pl.pallas_call(kernel, out_shape=(jax.ShapeDtypeStruct((TOK, D), BF), jax...  66.8 us
    pallas_call x1, Pallas kernels, local(): pl.pallas_call(finish, out_shape=tuple((jax.ShapeDtypeStruct(o.shape, o.d...  2.3 us

profile of v3, /device:TPU:57, one launch (start us, length us, event | category | flops | bytes accessed | tf_op | source)
XLA Modules:
  0.0 69.7 jit_solution(3898320571382158843)
XLA Ops:
  0.6 66.8 %relay.1 = (bf16[128,2048]{1,0:T(8,128)(2,1)}, bf16[128,2048]{1,0:T(8,128)(2,1)}, bf16[192,512]{1,0:T(8,128)(2,1)}, bf16[192,512]{1,0:T(8,128)(2,1)}, bf16[192,512]{1,0:T(8,128)(2,1)}, /*index=5*/f32[1,2048]{1,0:T(1,128)}) custom-call(bf16[128,2048]{1,0:T(8,128)(2,1)} %bitcast.25, bf16[128,2048]{1,0:T(8,128)(2,1)} %bitcast.26, bf16[128,2048]{1,0:T(8,128)(2,1)} %bitcast.27, ...), custom_call_target="tpu_custom_call" | custom-call | tf_op jit(solution)/shard_map/relay/pallas_call | solution.py:687
  67.4 2.3 %finish.1 = (bf16[128,2048]{1,0:T(8,128)(2,1)}, bf16[128,2048]{1,0:T(8,128)(2,1)}, bf16[192,512]{1,0:T(8,128)(2,1)}, bf16[192,512]{1,0:T(8,128)(2,1)}, bf16[192,512]{1,0:T(8,128)(2,1)}, /*index=5*/f32[1,2048]{1,0:T(1,128)}) custom-call(bf16[128,2048]{1,0:T(8,128)(2,1)} %get-tuple-element.18.refs_0_, bf16[128,2048]{1,0:T(8,128)(2,1)} %get-tuple-element.19.refs_1_, ...), custom_call_target="tpu_custom_call" | custom-call | tf_op jit(solution)/shard_map/finish/pallas_call | solution.py:750

commit v4 on v3

--- a/solution.py
+++ b/solution.py
@@ -205,11 +205,9 @@
             out_by(sc_ref, k, 2 * k).start()
 
     def out_up():
-        @pl.when(s == half - 1)
-        def _():
-            pl.semaphore_wait(ready, relays)
-            for k in range(relays):
-                out_by(so_ref, k, half + 1 + 2 * k).start()
+        pl.semaphore_wait(ready, relays)
+        for k in range(relays):
+            out_by(so_ref, k, half + 1 + 2 * k).start()
 
     def in_by(dst, k, section):
         first = k * step if isinstance(k, int) else pl.multiple_of(k * step, step)
@@ -306,7 +304,6 @@
     smalls[2].wait()
     rows[0, e] = normed_rows(pick_b, kept[...])
     z_own(0)
-    out_up()
     smalls[3].wait()
     smalls[4].wait()
     pick_f, _ = slots(fe_ref[...], fs_ref[...])
@@ -323,6 +320,7 @@
         hop_inc.wait_recv()
         rows[2, e] = normed_rows(pick_f, inc[...])
         z_own(2)
+        out_up()
 
     @pl.when(s == last)
     def _():
@@ -351,32 +349,46 @@
     def _():
         first_in.wait()
 
+    @pl.when(from_before & punctual)
+    def _():
+        hop_inc.wait_recv()
+
+    @pl.when(punctual & (s != half))
+    def _():
+        rows[2, e] = normed_rows(pick_f, inc[...])
+
+    @pl.when(outer & punctual & (s != half))
+    def _():
+        z_send(2, 0, near)
+
+    z_pass(1, (end, 2, other), (other, 3, end))
+    w_pass(2)
+
+    @pl.when(s != half)
+    def _():
+        z_pass(2, (end, 2, other))
+
+    @pl.when(inner & punctual & (s != half))
+    def _():
+        z_send(2, 0, other)
+
+    z_pass(1, (far, 4, end))
+
     @pl.when(s == half)
     def _():
         for k in range(relays):
             in_by(inc, k, half).wait_recv()
-
-    @pl.when(from_before & punctual)
-    def _():
-        hop_inc.wait_recv()
-
-    @pl.when(punctual)
-    def _():
         rows[2, e] = normed_rows(pick_f, inc[...])
 
-    @pl.when(outer & punctual)
-    def _():
-        z_send(2, 0, near)
-
-    z_pass(1, (end, 2, other), (other, 3, end))
-    w_pass(2)
-    z_pass(2, (end, 2, other))
-
-    @pl.when(inner & punctual)
-    def _():
-        z_send(2, 0, other)
-
-    z_pass(1, (far, 4, end))
+        @pl.when(outer)
+        def _():
+            z_send(2, 0, near)
+
+        z_pass(2, (end, 2, other))
+
+        @pl.when(inner)
+        def _():
+            z_send(2, 0, other)
 
     def z_arrived(a, block):
         for c in range(CA):
@@ -522,6 +534,22 @@
     for a in range(3):
         w_arrived(a)
 
+    gain_z = [remote(gst.at[0, 0], gst.at[0, d], gsend.at[0, d], grecv.at[0, d], (s, zs[d], r)) for d in (1, 2, 3)]
+    gain_x = [remote(gst.at[1, 0], gst.at[1, d], gsend.at[1, d], grecv.at[1, d], (s, e, xs[d])) for d in (1, 2, 3)]
+
+    def send_gain():
+        terms = part[0].reshape(4 * CAP, D).astype(F32) * rows[0].reshape(4 * CAP, D).astype(F32)
+        gst[0, 0] = jnp.sum(terms, axis=0, keepdims=True) / gain
+        for c in gain_z:
+            c.start()
+
+    def pass_gain():
+        for c in gain_z:
+            c.wait_recv()
+        gst[1, 0] = (gst[0, 0] + gst[0, 1]) + (gst[0, 2] + gst[0, 3])
+        for c in gain_x:
+            c.start()
+
     @pl.when(outer)
     def _():
         got[0, 2] = jnp.zeros((CAP, D), BF)
@@ -531,17 +559,20 @@
             z_arrived(1, block)
             backward_block(block)
             send_term(0, make)
-        backward_block(e)
+            if make is for_near:
+                backward_block(e)
         send_weight_grads()
+        send_gain()
         for block, make in ((3 - e, for_far), (3 - near, for_across), (near, for_near)):
             z_arrived(2, block)
             forward_block(block)
             send_term(1, make)
             if make is for_far:
                 send_weight_grads_near()
+                forward_block(e)
             if make is for_across:
                 join_weight_grads()
-        forward_block(e)
+                pass_gain()
 
     @pl.when(inner)
     def _():
@@ -551,6 +582,7 @@
         for k in range(4):
             part[0, :, :, k * DS : (k + 1) * DS] = backward_part(made[0], made[1], k).reshape(4, CAP, DS)
         send_weight_grads()
+        send_gain()
 
     z_pass(2, (far, 4, end))
     z_pass(2, (other, 3, end))
@@ -568,6 +600,7 @@
         pass_term(0, other, 1, for_across, on_other)
         join_weight_grads()
         pass_term(0, far, 0, for_far, on_far)
+        pass_gain()
         pass_term(0, end, 2, on_far, on_end)
         pass_term(1, far, 0, for_far, on_far)
 
@@ -577,12 +610,6 @@
     parts_arrived(0)
     grad_normed = dot_nn(table_b[:, : 3 * CAP], got[0].reshape(3 * CAP, D))
     xhat = kept[...].astype(F32) * rscale_b
-    gst[0, 0] = jnp.sum(grad_normed * xhat, axis=0, keepdims=True)
-    gain_z = []
-    for d in (1, 2, 3):
-        c = remote(gst.at[0, 0], gst.at[0, d], gsend.at[0, d], grecv.at[0, d], (s, zs[d], r))
-        c.start()
-        gain_z.append(c)
     gx = grad_normed * gain
     mean = jnp.mean(gx * xhat, axis=1, keepdims=True)
     ig[...] = (cot[...].astype(F32) + rscale_b * (gx - xhat * mean)).astype(BF)
@@ -593,15 +620,6 @@
     def _():
         pass_term(1, other, 1, for_across, on_other)
         pass_term(1, end, 2, on_far, on_end)
-
-    for c in gain_z:
-        c.wait_recv()
-    gst[1, 0] = (gst[0, 0] + gst[0, 1]) + (gst[0, 2] + gst[0, 3])
-    gain_x = []
-    for d in (1, 2, 3):
-        c = remote(gst.at[1, 0], gst.at[1, d], gsend.at[1, d], grecv.at[1, d], (s, e, xs[d]))
-        c.start()
-        gain_x.append(c)
 
     parts_arrived(1)
     tokens = dot_nn(table_f[:, : 3 * CAP], got[1].reshape(3 * CAP, D))
@@ -669,21 +687,17 @@
 
 
 def finish(*refs):
-    ins, outs, held, sems = refs[:6], refs[6:12], refs[12:18], refs[18]
-    loads = [pltpu.make_async_copy(ins[i], held[i], sems.at[0, i]) for i in range(6)]
-    stores = [pltpu.make_async_copy(held[i], outs[i], sems.at[1, i]) for i in range(6)]
-    for c in loads:
+    copies = [pltpu.make_async_copy(refs[i], refs[6 + i], refs[12].at[i]) for i in range(6)]
+    for c in copies:
         c.start()
-    for load, store in zip(loads, stores):
-        load.wait()
-        store.start()
-    for c in stores:
+    for c in copies:
         c.wait()
 
 
 def local(so, ft, kept, sc, lc, gain, gw, uw, dw, fe, fs, be, bs):
     any_spec = pl.BlockSpec(memory_space=pl.ANY)
     dma = pltpu.SemaphoreType.DMA
+    hbm = lambda x: pltpu.with_memory_space_constraint(x, pltpu.HBM)
     outs = pl.pallas_call(
         kernel,
         out_shape=(
@@ -740,22 +754,23 @@
             dma((2, 4)),
         ],
         compiler_params=pltpu.CompilerParams(
-            collective_id=0, has_side_effects=True, vmem_limit_bytes=60 << 20
+            collective_id=0, has_side_effects=True, vmem_limit_bytes=40 << 20
         ),
         name="relay",
     )(
-        so.reshape(TOK, D), ft.reshape(TOK, D), kept.reshape(TOK, D), sc.reshape(TOK, D), lc.reshape(TOK, D),
-        gain.reshape(1, D), gw[0], uw[0], dw[0], fe[0, 0].T, fs[0, 0].T, be[0, 0].T, bs[0, 0].T,
+        hbm(so.reshape(TOK, D)), hbm(ft.reshape(TOK, D)), hbm(kept.reshape(TOK, D)), hbm(sc.reshape(TOK, D)),
+        hbm(lc.reshape(TOK, D)), hbm(gain.reshape(1, D)), hbm(gw[0]), hbm(uw[0]), hbm(dw[0]),
+        hbm(fe[0, 0].T), hbm(fs[0, 0].T), hbm(be[0, 0].T), hbm(bs[0, 0].T),
     )
     outs = pl.pallas_call(
         finish,
         out_shape=tuple(jax.ShapeDtypeStruct(o.shape, o.dtype) for o in outs),
         in_specs=[any_spec] * 6,
         out_specs=[any_spec] * 6,
-        scratch_shapes=[pltpu.VMEM(o.shape, o.dtype) for o in outs] + [dma((2, 6))],
-        compiler_params=pltpu.CompilerParams(vmem_limit_bytes=60 << 20),
+        scratch_shapes=[dma((6,))],
+        compiler_params=pltpu.CompilerParams(vmem_limit_bytes=16 << 20),
         name="finish",
-    )(*outs)
+    )(*[pltpu.with_memory_space_constraint(o, pltpu.VMEM) for o in outs])
     return (
         outs[0][None, None], outs[1][None, None], outs[2][None], outs[3][None], outs[4][None], outs[5],
     )

time: 69.9 us -> 64.9 us (0.928)
  the two profiles are of different devices: /device:TPU:57 before, /device:TPU:1 now
where the time goes in v4:
time: 64.9 us; the launch traced here: 64.1 us
  Pallas kernels  63.4 us (98%)
  between operations  0.65 us (1%)
    pallas_call x1, Pallas kernels, local(): pl.pallas_call(kernel, out_shape=(jax.ShapeDtypeStruct((TOK, D), BF), jax...  62.2 us

profile of v4, /device:TPU:1, one launch (start us, length us, event | category | flops | bytes accessed | tf_op | source)
XLA Modules:
  0.0 64.1 jit_solution(2037587419121667678)
XLA Ops:
  0.6 62.2 %relay.1 = (bf16[128,2048]{1,0:T(8,128)(2,1)S(1)}, bf16[128,2048]{1,0:T(8,128)(2,1)S(1)}, bf16[192,512]{1,0:T(8,128)(2,1)S(1)}, bf16[192,512]{1,0:T(8,128)(2,1)S...) custom-call(bf16[128,2048]{1,0:T(8,128)(2,1)} %bitcast.25, bf16[128,2048]{1,0:T(8,128)(2,1)} %bitcast.26, ...), custom_call_target="tpu_custom_call" | custom-call | tf_op jit(solution)/shard_map/relay/pallas_call | solution.py:701
  62.9 1.2 %finish.1 = (bf16[128,2048]{1,0:T(8,128)(2,1)}, bf16[128,2048]{1,0:T(8,128)(2,1)}, bf16[192,512]{1,0:T(8,128)(2,1)}, bf16[192,512]{1,0:T(8,128)(2,1)}, bf16[192,512]{1,0:T(8,128)(2,1)}, /*index=5*/f32[1,2048]{1,0:T(1,128)}) custom-call(bf16[128,2048]{1,0:T(8,128)(2,1)S(1)} %get-tuple-element.18.refs_0_, bf16[128,2048]{1,0:T(8,128)(2,1)S(1)} %get-tuple-element.19.refs_1_, ...), custom_call_target="tpu_custom_call" | custom-call | tf_op jit(solution)/shard_map/finish/pallas_call | solution.py:765

commit v5 on v4

--- a/solution.py
+++ b/solution.py
@@ -621,13 +621,7 @@
         pass_term(1, other, 1, for_across, on_other)
         pass_term(1, end, 2, on_far, on_end)
 
-    parts_arrived(1)
-    tokens = dot_nn(table_f[:, : 3 * CAP], got[1].reshape(3 * CAP, D))
-    lo[...] = (inc[...].astype(F32) + scale_f * tokens).astype(BF)
-    out_lo = pltpu.make_async_copy(lo, lo_ref, osem.at[1])
-    out_lo.start()
-    outs = [out_ig, out_lo]
-
+    outs = [out_ig]
     for a, ref in enumerate((gg_ref, ug_ref, dg_ref)):
         for h in range(2):
             d_near(a, h, False).wait_recv()
@@ -637,6 +631,13 @@
         c = pltpu.make_async_copy(dwout.at[a], ref, osem.at[2 + a])
         c.start()
         outs.append(c)
+    parts_arrived(1)
+    tokens = dot_nn(table_f[:, : 3 * CAP], got[1].reshape(3 * CAP, D))
+    lo[...] = (inc[...].astype(F32) + scale_f * tokens).astype(BF)
+    out_lo = pltpu.make_async_copy(lo, lo_ref, osem.at[1])
+    out_lo.start()
+    outs.append(out_lo)
+
     for c in gain_x:
         c.wait_recv()
     gout[...] = (gst[1, 0] + gst[1, 1]) + (gst[1, 2] + gst[1, 3])

time: 64.9 us -> 65.2 us (level)
  no operation moved by 1% of the time
where the time goes in v5:
time: 65.2 us; the launch traced here: 64.1 us
  Pallas kernels  63.4 us (97%)
    pallas_call x1, Pallas kernels, local(): pl.pallas_call(kernel, out_shape=(jax.ShapeDtypeStruct((TOK, D), BF), jax...  62.2 us

profile of v5, /device:TPU:1, one launch (start us, length us, event | category | flops | bytes accessed | tf_op | source)
XLA Modules:
  0.0 64.1 jit_solution(6192864634288593015)
XLA Ops:
  0.6 62.2 %relay.1 = (bf16[128,2048]{1,0:T(8,128)(2,1)S(1)}, bf16[128,2048]{1,0:T(8,128)(2,1)S(1)}, bf16[192,512]{1,0:T(8,128)(2,1)S(1)}, bf16[192,512]{1,0:T(8,128)(2,1)S...) custom-call(bf16[128,2048]{1,0:T(8,128)(2,1)} %bitcast.25, bf16[128,2048]{1,0:T(8,128)(2,1)} %bitcast.26, ...), custom_call_target="tpu_custom_call" | custom-call | tf_op jit(solution)/shard_map/relay/pallas_call | solution.py:702
  62.9 1.2 %finish.1 = (bf16[128,2048]{1,0:T(8,128)(2,1)}, bf16[128,2048]{1,0:T(8,128)(2,1)}, bf16[192,512]{1,0:T(8,128)(2,1)}, bf16[192,512]{1,0:T(8,128)(2,1)}, bf16[192,512]{1,0:T(8,128)(2,1)}, /*index=5*/f32[1,2048]{1,0:T(1,128)}) custom-call(bf16[128,2048]{1,0:T(8,128)(2,1)S(1)} %get-tuple-element.18.refs_0_, bf16[128,2048]{1,0:T(8,128)(2,1)S(1)} %get-tuple-element.19.refs_1_, ...), custom_call_target="tpu_custom_call" | custom-call | tf_op jit(solution)/shard_map/finish/pallas_call | solution.py:766

commit v6 on v5

--- a/solution.py
+++ b/solution.py
@@ -601,8 +601,8 @@
         join_weight_grads()
         pass_term(0, far, 0, for_far, on_far)
         pass_gain()
+        pass_term(1, far, 0, for_far, on_far)
         pass_term(0, end, 2, on_far, on_end)
-        pass_term(1, far, 0, for_far, on_far)
 
     got[0, 0] = part[0, e]
     got[1, 0] = part[1, e]

time: 65.2 us -> 65.2 us (level)
  no operation moved by 1% of the time
where the time goes in v6:
time: 65.2 us; the launch traced here: 64.1 us
  Pallas kernels  63.4 us (97%)
    pallas_call x1, Pallas kernels, local(): pl.pallas_call(kernel, out_shape=(jax.ShapeDtypeStruct((TOK, D), BF), jax...  62.2 us

profile of v6, /device:TPU:1, one launch (start us, length us, event | category | flops | bytes accessed | tf_op | source)
XLA Modules:
  0.0 64.1 jit_solution(8068533020266912865)
XLA Ops:
  0.6 62.2 %relay.1 = (bf16[128,2048]{1,0:T(8,128)(2,1)S(1)}, bf16[128,2048]{1,0:T(8,128)(2,1)S(1)}, bf16[192,512]{1,0:T(8,128)(2,1)S(1)}, bf16[192,512]{1,0:T(8,128)(2,1)S...) custom-call(bf16[128,2048]{1,0:T(8,128)(2,1)} %bitcast.25, bf16[128,2048]{1,0:T(8,128)(2,1)} %bitcast.26, ...), custom_call_target="tpu_custom_call" | custom-call | tf_op jit(solution)/shard_map/relay/pallas_call | solution.py:702
  62.9 1.2 %finish.1 = (bf16[128,2048]{1,0:T(8,128)(2,1)}, bf16[128,2048]{1,0:T(8,128)(2,1)}, bf16[192,512]{1,0:T(8,128)(2,1)}, bf16[192,512]{1,0:T(8,128)(2,1)}, bf16[192,512]{1,0:T(8,128)(2,1)}, /*index=5*/f32[1,2048]{1,0:T(1,128)}) custom-call(bf16[128,2048]{1,0:T(8,128)(2,1)S(1)} %get-tuple-element.18.refs_0_, bf16[128,2048]{1,0:T(8,128)(2,1)S(1)} %get-tuple-element.19.refs_1_, ...), custom_call_target="tpu_custom_call" | custom-call | tf_op jit(solution)/shard_map/finish/pallas_call | solution.py:766
